TPU v7x, 128 devices: a whole 4x4x4 slice. The times are simulated.
128 devices in a mesh: member: 8 (over x, core), slab: 16 (over z, y).
Axes of the slice: x: 4, y: 4, z: 4, core: 2. Of those that a mesh axis runs over, the one named last changes fastest.
Arguments:
- nonnegative_volumes: float32 [8, 64, 128, 128], P('member', 'slab'), may hold values from 0.25 to 4
- reaction: float32 [64, 128, 128], P('slab'), may hold values from 0.02 to 0.2
- diffusivity: float32 [3], replicated, may hold values from 4 to 32
- member_weights: float32 [8], P('member'), may hold values from 0.5 to 2
Outputs:
- wasserstein_centroid: float32 [64, 128, 128], P('slab')
- final_multipliers: float32 [8, 64, 128, 128], P('member', 'slab')
All inputs are finite; a program needn't handle non-finite values.
Results may differ from a plain program's by a relative error of at most 0.0001.
Values sent between devices are 32-bit elements; how exact they have to be, the bound alone decides.
A program may use at most 128 MiB of HBM per device.

v0:
```python
import jax
import jax.numpy as jnp
from jax import lax
from jax.sharding import PartitionSpec as P

ITERS = 3
LEVELS = 4
POST = 2
COARSE_SWEEPS = 8


OMEGA = 0.8


def with_halo(cells, sides, width):
    for axis, dim in sides:
        count = lax.axis_size(axis)
        ends = count - 1
        head = lax.slice_in_dim(cells, 0, width, axis=dim)
        tail = lax.slice_in_dim(cells, cells.shape[dim] - width, cells.shape[dim], axis=dim)
        cells = jnp.concatenate(
            [
                lax.ppermute(tail, axis, [(i, (i + 1) % count) for i in range(ends)]),
                cells,
                lax.ppermute(head, axis, [((i + 1) % count, i) for i in range(ends)]),
            ],
            axis=dim,
        )
    return cells


def restrict(array):
    zdim, ydim, xdim = array.shape
    folded = array.reshape(zdim // 2, 2, ydim, xdim)
    summed = folded[:, 0] + folded[:, 1]
    folded = summed.reshape(zdim // 2, ydim // 2, 2, xdim)
    summed = folded[:, :, 0] + folded[:, :, 1]
    folded = summed.reshape(zdim // 2, ydim // 2, xdim // 2, 2)
    summed = folded[..., 0] + folded[..., 1]
    return summed * 0.125


def prolong(array):
    zdim, ydim, xdim = array.shape
    spread = jnp.broadcast_to(array[:, None, :, None, :, None], (zdim, 2, ydim, 2, xdim, 2))
    return spread.reshape(2 * zdim, 2 * ydim, 2 * xdim)


def stencil(padded, reaction_level, coupling):
    field = padded[1:-1]
    padded_side = jnp.pad(field, ((0, 0), (1, 1), (1, 1)))
    second_z = 2.0 * field - padded[2:] - padded[:-2]
    second_y = 2.0 * field - padded_side[:, 2:, 1:-1] - padded_side[:, :-2, 1:-1]
    second_x = 2.0 * field - padded_side[:, 1:-1, 2:] - padded_side[:, 1:-1, :-2]
    return (
        reaction_level * field
        + coupling[0] * second_z
        + coupling[1] * second_y
        + coupling[2] * second_x
    )


def apply_operator(field, multigrid_depth, reactions, couplings):
    if multigrid_depth == 0:
        padded = with_halo(field, (("slab", 0),), 1)
    elif multigrid_depth == 1:
        padded = with_halo(field, (("slab", 0),), 1)
    else:
        padded = jnp.pad(field, ((1, 1), (0, 0), (0, 0)))
    return stencil(padded, reactions[multigrid_depth], couplings[multigrid_depth])


def vcycle(source, multigrid_depth, reactions, couplings, diagonals, first_shared, slab_index):
    diagonal = diagonals[multigrid_depth]
    iterate = OMEGA * source / diagonal
    if multigrid_depth == LEVELS - 1:
        for repeat in range(COARSE_SWEEPS - 1):
            iterate = (
                iterate
                + OMEGA
                * (source - apply_operator(iterate, multigrid_depth, reactions, couplings))
                / diagonal
            )
        return iterate
    iterate = (
        iterate
        + OMEGA
        * (source - apply_operator(iterate, multigrid_depth, reactions, couplings))
        / diagonal
    )
    residual = source - apply_operator(iterate, multigrid_depth, reactions, couplings)
    coarsened_grid = restrict(residual)
    if multigrid_depth + 1 == first_shared:
        planes = coarsened_grid.shape[0]
        coarsened_grid = lax.all_gather(coarsened_grid, "slab", axis=0, tiled=True)
        correction = vcycle(
            coarsened_grid,
            multigrid_depth + 1,
            reactions,
            couplings,
            diagonals,
            first_shared,
            slab_index,
        )
        correction = lax.dynamic_slice_in_dim(correction, slab_index * planes, planes, 0)
    else:
        correction = vcycle(
            coarsened_grid,
            multigrid_depth + 1,
            reactions,
            couplings,
            diagonals,
            first_shared,
            slab_index,
        )
    iterate = iterate + prolong(correction)
    for repeat in range(POST):
        iterate = (
            iterate
            + OMEGA
            * (source - apply_operator(iterate, multigrid_depth, reactions, couplings))
            / diagonal
        )
    return iterate


def body(nonnegative_volumes, reaction, diffusivity, member_weights):
    slab_index = lax.axis_index("slab")
    first_shared = 2
    reactions = [reaction]
    reactions.append(restrict(reactions[-1]))
    shared_reaction = lax.all_gather(restrict(reactions[-1]), "slab", axis=0, tiled=True)
    reactions.append(shared_reaction)
    multigrid_depth = 3
    reactions.append(restrict(reactions[-1]))
    couplings = [diffusivity * 0.25**multigrid_depth for multigrid_depth in range(LEVELS)]
    diagonals = [
        reactions[multigrid_depth]
        + 2.0
        * (
            couplings[multigrid_depth][0]
            + couplings[multigrid_depth][1]
            + couplings[multigrid_depth][2]
        )
        for multigrid_depth in range(LEVELS)
    ]

    def gibbs_smoother(source):
        return vcycle(source, 0, reactions, couplings, diagonals, first_shared, slab_index)

    supplied_volume = nonnegative_volumes[0]
    own_weight = member_weights[0]
    weight_total = lax.psum(jnp.sum(member_weights), "member")
    final_multipliers = jnp.ones_like(supplied_volume)
    wasserstein_centroid = jnp.zeros_like(supplied_volume)
    for repeat in range(ITERS):
        companion_multiplier = supplied_volume / gibbs_smoother(final_multipliers)
        desired_mass_vector = final_multipliers * gibbs_smoother(companion_multiplier)
        weighted_log = own_weight * jnp.log(desired_mass_vector)
        log_total = lax.psum(weighted_log, "member")
        wasserstein_centroid = jnp.exp(log_total / weight_total)
        final_multipliers = final_multipliers * wasserstein_centroid / desired_mass_vector
    return (wasserstein_centroid, final_multipliers[None])


def solution(mesh):
    placed = (P("member", "slab", None, None), P("slab", None, None), P(), P("member"))
    return jax.shard_map(
        body,
        mesh=mesh,
        in_specs=placed,
        out_specs=(P("slab", None, None), P("member", "slab", None, None)),
        check_vma=False,
    )
```

profile of v0, /device:TPU:1, one launch (start us, length us, event | category | flops | bytes accessed | tf_op | source)
XLA Modules:
  0.0 1259.8 jit_solution(1493901794437919200)
XLA Ops:
  12.9 4.7 collective-permute-start.1
  44.0 26.2 %all-gather.1 = f32[16,32,32,1]{2,1,3,0:T(8,128)S(1)} all-gather(f32[1,32,32,1]{2,1,3,0:T(8,128)S(1)} %add_multiply_fusion.6), channel_id=3, replica_groups=mesh['member'=8,'slab'=16] {'slab'}, dimensions={0}, use_global_device_ids=true | all-gather | bytes 69632 | tf_op jit(solution)/shard_map/all_gather | solution.py:132
  81.1 20.4 %all-gather = f32[16,32,32,1]{2,1,3,0:T(8,128)S(1)} all-gather(f32[1,32,32,1]{2,1,3,0:T(8,128)S(1)} %add_multiply_fusion.7), channel_id=2, replica_groups=mesh['member'=8,'slab'=16] {'slab'}, dimensions={0}, use_global_device_ids=true | all-gather | bytes 69632 | tf_op jit(solution)/shard_map/all_gather | solution.py:95
  148.1 6.6 broadcast_in_dim.156
  154.7 12.6 %reshape.876 = f32[4,128,128]{2,1,0:T(8,128)S(1)} reshape(f32[2,2,64,2,64,2]{5,4,3,2,1,0:T(8,128)} %broadcast_in_dim.156) | data formatting | bytes 524288 | tf_op jit(solution)/shard_map/reshape | solution.py:46
  177.8 4.3 collective-permute-start.15
  187.0 5.7 collective-permute-start.17
  197.5 6.6 collective-permute-start.19
  209.1 6.4 collective-permute-start.21
  219.8 6.4 collective-permute-start.23
  229.6 28.9 %all-gather.2 = f32[16,32,32,1]{2,1,3,0:T(8,128)S(1)} all-gather(f32[1,32,32,1]{2,1,3,0:T(8,128)S(1)} %add_multiply_fusion.5), channel_id=4, replica_groups=mesh['member'=8,'slab'=16] {'slab'}, dimensions={0}, use_global_device_ids=true | all-gather | bytes 69632 | tf_op jit(solution)/shard_map/all_gather | solution.py:95
  305.3 6.6 broadcast_in_dim.162
  311.9 12.6 %reshape.881 = f32[4,128,128]{2,1,0:T(8,128)S(1)} reshape(f32[2,2,64,2,64,2]{5,4,3,2,1,0:T(8,128)} %broadcast_in_dim.162) | data formatting | bytes 524288 | tf_op jit(solution)/shard_map/reshape | solution.py:46
  334.9 4.3 collective-permute-start.31
  343.6 46.1 %psum.29 = f32[]{:T(128)} all-reduce(f32[]{:T(128)} %bitcast), channel_id=1, replica_groups=mesh['member'=8,'slab'=16] {'member'}, use_global_device_ids=true, to_apply=%region_1.0 | all-reduce | flops 1 | bytes 8 | tf_op jit(solution)/shard_map/psum | solution.py:153
  389.7 52.7 %all-reduce.184.cloned.1.call-done = f32[4,128,128]{2,1,0:T(8,128)} async-done(((f32[4,128,128]{2,1,0:T(8,128)}), f32[4,128,128]{2,1,0:T(8,128)}) %all-reduce.184.cloned.1.call-update) | async-done | bytes 262160 | tf_op jit(solution)/shard_map/psum | solution.py:160
  454.2 4.3 collective-permute-start.35
  463.6 4.3 collective-permute-start.37
  472.3 4.4 collective-permute-start.39
  480.1 30.0 %all-gather.3 = f32[16,32,32,1]{2,1,3,0:T(8,128)S(1)} all-gather(f32[1,32,32,1]{2,1,3,0:T(8,128)S(1)} %add_multiply_fusion.4), channel_id=5, replica_groups=mesh['member'=8,'slab'=16] {'slab'}, dimensions={0}, use_global_device_ids=true | all-gather | bytes 69632 | tf_op jit(solution)/shard_map/all_gather | solution.py:95
  556.7 6.6 broadcast_in_dim.168
  563.3 12.6 %reshape.886 = f32[4,128,128]{2,1,0:T(8,128)S(1)} reshape(f32[2,2,64,2,64,2]{5,4,3,2,1,0:T(8,128)} %broadcast_in_dim.168) | data formatting | bytes 524288 | tf_op jit(solution)/shard_map/reshape | solution.py:46
  586.4 4.3 collective-permute-start.47
  595.6 4.3 collective-permute-start.49
  604.7 6.2 collective-permute-start.51
  616.0 6.4 collective-permute-start.53
  626.8 6.4 collective-permute-start.55
  636.6 29.4 %all-gather.4 = f32[16,32,32,1]{2,1,3,0:T(8,128)S(1)} all-gather(f32[1,32,32,1]{2,1,3,0:T(8,128)S(1)} %add_multiply_fusion.3), channel_id=6, replica_groups=mesh['member'=8,'slab'=16] {'slab'}, dimensions={0}, use_global_device_ids=true | all-gather | bytes 69632 | tf_op jit(solution)/shard_map/all_gather | solution.py:95
  712.7 6.6 broadcast_in_dim.174
  719.3 12.6 %reshape.891 = f32[4,128,128]{2,1,0:T(8,128)S(1)} reshape(f32[2,2,64,2,64,2]{5,4,3,2,1,0:T(8,128)} %broadcast_in_dim.174) | data formatting | bytes 524288 | tf_op jit(solution)/shard_map/reshape | solution.py:46
  742.3 4.3 collective-permute-start.63
  751.0 95.4 %all-reduce.186.cloned.1.call-done = f32[4,128,128]{2,1,0:T(8,128)} async-done(((f32[4,128,128]{2,1,0:T(8,128)}), f32[4,128,128]{2,1,0:T(8,128)}) %all-reduce.186.cloned.1.call-update) | async-done | bytes 262160 | tf_op jit(solution)/shard_map/psum | solution.py:160
  858.2 4.3 collective-permute-start.67
  867.7 4.3 collective-permute-start.69
  876.3 4.4 collective-permute-start.71
  884.1 29.8 %all-gather.5 = f32[16,32,32,1]{2,1,3,0:T(8,128)S(1)} all-gather(f32[1,32,32,1]{2,1,3,0:T(8,128)S(1)} %add_multiply_fusion.2), channel_id=7, replica_groups=mesh['member'=8,'slab'=16] {'slab'}, dimensions={0}, use_global_device_ids=true | all-gather | bytes 69632 | tf_op jit(solution)/shard_map/all_gather | solution.py:95
  960.6 6.6 broadcast_in_dim.180
  967.2 12.6 %reshape.896 = f32[4,128,128]{2,1,0:T(8,128)S(1)} reshape(f32[2,2,64,2,64,2]{5,4,3,2,1,0:T(8,128)} %broadcast_in_dim.180) | data formatting | bytes 524288 | tf_op jit(solution)/shard_map/reshape | solution.py:46
  990.3 4.3 collective-permute-start.79
  999.4 4.3 collective-permute-start.81
  1008.6 6.2 collective-permute-start.83
  1019.9 6.4 collective-permute-start.85
  1030.6 6.4 collective-permute-start.87
  1040.5 29.5 %all-gather.6 = f32[16,32,32,1]{2,1,3,0:T(8,128)S(1)} all-gather(f32[1,32,32,1]{2,1,3,0:T(8,128)S(1)} %add_multiply_fusion.1), channel_id=8, replica_groups=mesh['member'=8,'slab'=16] {'slab'}, dimensions={0}, use_global_device_ids=true | all-gather | bytes 69632 | tf_op jit(solution)/shard_map/all_gather | solution.py:95
  1116.6 6.6 broadcast_in_dim.186
  1123.2 12.6 %reshape.901 = f32[4,128,128]{2,1,0:T(8,128)S(1)} reshape(f32[2,2,64,2,64,2]{5,4,3,2,1,0:T(8,128)} %broadcast_in_dim.186) | data formatting | bytes 524288 | tf_op jit(solution)/shard_map/reshape | solution.py:46
  1146.3 4.3 collective-permute-start.95
  1154.9 95.5 %all-reduce.188.cloned.1.call-done = f32[4,128,128]{2,1,0:T(8,128)} async-done(((f32[4,128,128]{2,1,0:T(8,128)}), f32[4,128,128]{2,1,0:T(8,128)}) %all-reduce.188.cloned.1.call-update) | async-done | bytes 262160 | tf_op jit(solution)/shard_map/psum | solution.py:160
  (544 shorter events, 506.8 us)
Async XLA Ops:
  7.2 435.2 %all-reduce.184.cloned.1.call-start = ((), (), s32[]{:S(2)}) async-start(), calls=%async_computation | async-start | bytes 524288 | tf_op jit(solution)/shard_map/psum | solution.py:160
  11.6 10.5 collective-permute-start
  12.9 9.2 collective-permute-start.1
  25.2 9.6 collective-permute-start.2
  26.5 8.3 collective-permute-start.3
  38.7 31.7 %collective-permute-start.4 = (f32[1,64,64]{1,2,0:T(8,128)S(1)}, f32[1,64,64]{1,2,0:T(8,128)S(1)}, u32[]{:S(2)}, u32[]{:S(2)}) collective-permute-start(f32[1,64,64]{1,2,0:T(8,128)S(1)} %get-tuple-element.183), channel_id=1, source_target_pairs={{1,0},{2,1},{3,2},{4,3},{5,4},{6,5},{7,6},{8,7},{9,8},{10,9},{11,1... | collective-permute-start | bytes 49160 | tf_op jit(solution)/shard_map/ppermute | solution.py:25
  40.0 30.4 %collective-permute-start.5 = (f32[1,64,64]{1,2,0:T(8,128)S(1)}, f32[1,64,64]{1,2,0:T(8,128)S(1)}, u32[]{:S(2)}, u32[]{:S(2)}) collective-permute-start(f32[1,64,64]{1,2,0:T(8,128)S(1)} %get-tuple-element.184), channel_id=1, source_target_pairs={{0,1},{1,2},{2,3},{3,4},{4,5},{5,6},{6,7},{7,8},{8,9},{9,10},{10,1... | collective-permute-start | bytes 49160 | tf_op jit(solution)/shard_map/ppermute | solution.py:23
  176.5 5.6 collective-permute-start.14
  177.8 5.6 collective-permute-start.15
  185.7 7.0 collective-permute-start.16
  187.0 7.1 collective-permute-start.17
  196.2 7.9 collective-permute-start.18
  197.5 7.7 collective-permute-start.19
  207.8 7.7 collective-permute-start.20
  209.1 7.4 collective-permute-start.21
  218.5 7.7 collective-permute-start.22
  219.8 7.4 collective-permute-start.23
  333.6 6.3 collective-permute-start.30
  334.9 5.6 collective-permute-start.31
  343.5 502.9 %all-reduce.186.cloned.1.call-start = ((), (), s32[]{:S(2)}) async-start(), calls=%async_computation.1 | async-start | bytes 524288 | tf_op jit(solution)/shard_map/psum | solution.py:160
  452.9 5.6 collective-permute-start.34
  454.2 5.6 collective-permute-start.35
  471.0 5.7 collective-permute-start.38
  585.1 5.6 collective-permute-start.46
  586.4 5.6 collective-permute-start.47
  594.3 5.6 collective-permute-start.48
  595.6 5.6 collective-permute-start.49
  603.4 7.5 collective-permute-start.50
  604.7 7.5 collective-permute-start.51
  614.7 7.7 collective-permute-start.52
  616.0 7.4 collective-permute-start.53
  625.5 7.7 collective-permute-start.54
  626.8 7.4 collective-permute-start.55
  741.0 5.6 collective-permute-start.62
  742.3 5.6 collective-permute-start.63
  750.9 499.4 %all-reduce.188.cloned.1.call-start = ((), (), s32[]{:S(2)}) async-start(), calls=%async_computation.2 | async-start | bytes 524288 | tf_op jit(solution)/shard_map/psum | solution.py:160
  856.9 5.6 collective-permute-start.66
  858.2 5.6 collective-permute-start.67
  875.0 5.7 collective-permute-start.70
  990.3 5.6 collective-permute-start.79
  999.4 5.6 collective-permute-start.81
  1007.3 7.5 collective-permute-start.82
  1008.6 7.5 collective-permute-start.83
  1018.6 7.7 collective-permute-start.84
  1019.9 7.4 collective-permute-start.85
  1029.3 7.7 collective-permute-start.86
  1030.6 7.4 collective-permute-start.87
  1146.3 5.6 collective-permute-start.95
  (53 other events, 336.9 us)
Sparse Core Ops, SparseCore 0:
  343.6 98.6 all-reduce.183
  751.0 95.2 all-reduce.185
  1155.0 95.2 all-reduce.187
where the time goes:
time: 1280 us; the launch traced here: 1260 us
  waiting for transfers between devices  294 us (23%)
  starting transfers between devices  286 us (22%)
  other arithmetic  249 us (19%)
  blocking collectives  240 us (19%)
  local copies, waits for them, and re-layouts  165 us (13%)
  between operations  25.4 us (2%)
    psum x3, waiting for transfers between devices, body(): log_total = lax.psum(weighted_log, 'member')  244 us
    ppermute x48, starting transfers between devices, with_halo(): lax.ppermute(tail, axis, [(i, (i + 1) % count) for i in range(ends)])  224 us
    add x84, other arithmetic, vcycle(): iterate + OMEGA * (source - apply_operator(iterate, multigrid_depth, reac...  172 us
    all_gather x6, blocking collectives, vcycle(): coarsened_grid = lax.all_gather(coarsened_grid, 'slab', axis=0, tiled=True)  168 us
    reshape x12, local copies, waits for them, and re-layouts, prolong(): return spread.reshape(2 * zdim, 2 * ydim, 2 * xdim)  97.6 us
    ppermute x48, starting transfers between devices, with_halo(): lax.ppermute(head, axis, [((i + 1) % count, i) for i in range(ends)])  62 us
    broadcast_in_dim x30, local copies, waits for them, and re-layouts, prolong(): jnp.broadcast_to(array[:, None, :, None, :, None], (zdim, 2, ydim, 2, xdi...  59 us
    ppermute x48, waiting for transfers between devices, with_halo(): lax.ppermute(tail, axis, [(i, (i + 1) % count) for i in range(ends)])  50.5 us
  transfers between devices with their start and end apart: 99, of which 48 were waited for; matrix products, arithmetic and copies ran while one was open for 0% of the time, Pallas kernels for 0%

commit v1 on v0

v1 whole, which is shorter than its diff:
```python
import jax
import jax.numpy as jnp
from jax import lax
from jax.experimental import pallas as pl
from jax.experimental.pallas import tpu as pltpu
from jax.sharding import PartitionSpec as P

ITERS = 3
COARSE_SWEEPS = 8
OMEGA = 0.8
LANES = 128
NZ, NY = 64, 128
F32 = jnp.float32
MESH = pl.DeviceIdType.MESH
DIRECTIONS = ((-1, 0), (1, 0), (0, -1), (0, 1), (-1, -1), (-1, 1), (1, -1), (1, 1))

GEOMETRY = (
    dict(own_z=4, own_y=16, nz=16, ny=32, hz=3, planes=24, rows=64),
    dict(own_z=5, own_y=16, nz=8, ny=16, hz=4, planes=18, rows=48),
)


def dot(a, b):
    return jnp.dot(a, b, precision=lax.Precision.HIGHEST, preferred_element_type=F32)


def flat(a):
    return a.reshape(-1, LANES)


def lane_roll(a, shift):
    return pltpu.roll(flat(a), shift % LANES, 1).reshape(a.shape)


def kernel(
    vol_ref, reaction_ref, diff_ref, weight_ref, cent_out, mult_out,
    S0, D0, DG0, U0a, U0b, C0, T0,
    S1, D1, DG1, U1a, U1b, C1, T1,
    G, S2, D2, DG2, U2, T2, C2, D3,
    VB, MB, LB, XB, HB, PB, CB, WS, WB, IW,
    Rx, Rx1, R3a, R3b, P3a, P3b, PM, P0, PP, Px,
    h0_send, h0_recv, h1_send, h1_recv, g_send, g_recv,
    ra_send, ra_recv, va_send, va_recv, w_send, w_recv,
    x_send, x_recv, p_send, p_recv, c_send, c_recv, f_send, f_recv, o_send, o_recv,
):
    member, slab = lax.axis_index("member"), lax.axis_index("slab")
    cz, cy = slab // 4, lax.rem(slab, 4)
    mx, mc = member // 2, lax.rem(member, 2)

    def at_slab(dz, dy):
        return lax.rem(cz + dz + 4, 4) * 4 + lax.rem(cy + dy + 4, 4)

    def remote(src, dst, send, recv, to):
        return pltpu.make_async_remote_copy(
            src_ref=src, dst_ref=dst, send_sem=send, recv_sem=recv, device_id=to, device_id_type=MESH
        )

    barrier = pltpu.get_barrier_semaphore()
    for d in range(1, 16):
        pl.semaphore_signal(barrier, inc=1, device_id=(member, at_slab(d // 4, d % 4)), device_id_type=MESH)
    for d in range(1, 8):
        pl.semaphore_signal(barrier, inc=1, device_id=(lax.rem(member + d, 8), slab), device_id_type=MESH)
    pl.semaphore_wait(barrier, 22)

    def halo(level, slot):
        g = GEOMETRY[level]
        ref, send, recv = ((S0, h0_send, h0_recv), (S1, h1_send, h1_recv))[level]
        copies = []
        for k, (dz, dy) in enumerate(DIRECTIONS):
            oz, oy, nz, ny, hz = g["own_z"], g["own_y"], g["nz"], g["ny"], g["hz"]
            zs, zn, zd = {-1: (oz, hz, oz + nz), 0: (oz, nz, oz), 1: (oz + nz - hz, hz, oz - hz)}[dz]
            ys, yn, yd = {-1: (oy, 8, oy + ny), 0: (oy, ny, oy), 1: (oy + ny - 8, 8, oy - 8)}[dy]
            copies.append(
                remote(
                    ref.at[slot, pl.ds(zs, zn), pl.ds(ys, yn)],
                    ref.at[slot, pl.ds(zd, zn), pl.ds(yd, yn)],
                    send.at[slot, k], recv.at[slot, k], (member, at_slab(dz, dy)),
                )
            )
        return copies

    def gather(slot):
        return [
            remote(G.at[slot, slab], G.at[slot, slab], g_send.at[slot, d], g_recv.at[slot, d], (member, at_slab(d // 4, d % 4)))
            for d in range(1, 16)
        ]

    def begin(copies):
        for c in copies:
            c.start()

    def finish(copies):
        for c in copies:
            c.wait()

    def to_blocks(src, dst, dst_z, dst_y, send, recv):
        copies = []
        for d in range(1, 4):
            to = lax.rem(cy + d, 4)
            copies.append(
                remote(
                    src.at[:, pl.ds(pl.multiple_of(32 * to, 32), 32)],
                    dst.at[pl.ds(dst_z + 4 * cy, 4), pl.ds(dst_y, 32)],
                    send.at[d - 1], recv.at[d - 1], (member, cz * 4 + to),
                )
            )
        return copies

    def to_slabs(src, src_z, src_y, dst, send, recv):
        copies = []
        for d in range(1, 4):
            to = lax.rem(cy + d, 4)
            copies.append(
                remote(
                    src.at[pl.ds(src_z + 4 * to, 4), pl.ds(src_y, 32)],
                    dst.at[:, pl.ds(pl.multiple_of(32 * cy, 32), 32)],
                    send.at[d - 1], recv.at[d - 1], (member, cz * 4 + to),
                )
            )
        return copies

    reaction_moves = to_blocks(reaction_ref, S0.at[1], 4, 16, ra_send, ra_recv)
    volume_moves = to_blocks(vol_ref, VB, 0, 0, va_send, va_recv)
    begin(reaction_moves)
    begin(volume_moves)
    WS[...] = jnp.full((8, LANES), weight_ref[0], F32)
    weight_moves = [
        remote(WS, WB.at[d], w_send.at[d - 1], w_recv.at[d - 1], (lax.rem(member + d, 8), slab)) for d in range(1, 8)
    ]
    begin(weight_moves)

    coupling = [[diff_ref[i] * (0.25**level) for i in range(3)] for level in range(4)]
    center = [2.0 * (c[0] + c[1] + c[2]) for c in coupling]

    lane = lax.broadcasted_iota(jnp.int32, (1, LANES), 1)
    one, zero = jnp.ones((1, LANES), F32), jnp.zeros((1, LANES), F32)

    def lane_mask(keep):
        return jnp.where(keep, one, zero)

    row_i = lax.broadcasted_iota(jnp.int32, (LANES, LANES), 0)
    col_i = lax.broadcasted_iota(jnp.int32, (LANES, LANES), 1)

    def half(a):
        return lax.shift_right_logical(a, 1)

    def matrix(keep, value=1.0):
        return jnp.where(keep, jnp.full((LANES, LANES), value, F32), jnp.zeros((LANES, LANES), F32))

    col_chunk, col_in = col_i & ~31, col_i & 31
    row_chunk, row_in = row_i & ~31, row_i & 31
    Rx[...] = matrix(half(row_i) == col_i, 0.125)
    Rx1[...] = matrix((row_i < 64) & (half(row_i) + 32 * cz == col_i), 0.125)
    R3a[...] = matrix(row_chunk + half(row_in) == col_i, 0.125)
    R3b[...] = matrix(row_chunk + 16 + half(row_in) == col_i, 0.125)
    P3a[...] = matrix(row_i == col_chunk + half(col_in))
    P3b[...] = matrix(row_i == col_chunk + 16 + half(col_in))
    widen = (col_i < 64)
    PM[...] = matrix(widen & (row_i == half(col_i) + 32 * (cz - 1)) & (row_i >= 0))
    P0[...] = matrix(widen & (row_i == half(col_i) + 32 * cz))
    PP[...] = matrix(widen & (row_i == half(col_i) + 32 * (cz + 1)))
    Px[...] = matrix(row_i == half(col_i))

    left = [lane_mask(lane > 0) * coupling[0][2], None, lane_mask((lane & 31) > 0) * coupling[2][2], lane_mask((lane & 15) > 0) * coupling[3][2]]
    right = [lane_mask(lane < 127) * coupling[0][2], None, lane_mask((lane & 31) < 31) * coupling[2][2], lane_mask((lane & 15) < 15) * coupling[3][2]]

    for ref in (U0a, U0b):
        ref[:, 0:8, :] = jnp.zeros((24, 8, LANES), F32)
        ref[:, 56:64, :] = jnp.zeros((24, 8, LANES), F32)
    for ref in (U1a, U1b):
        ref[:, 0:8, :] = jnp.zeros((18, 8, LANES), F32)
        ref[:, 40:48, :] = jnp.zeros((18, 8, LANES), F32)
    U2[:, 0:8, :] = jnp.zeros((4, 8, LANES), F32)
    U2[:, 40:48, :] = jnp.zeros((4, 8, LANES), F32)
    S0[0, 1:23, 8:56, :] = jnp.ones((22, 48, LANES), F32)

    def neighbours(level, u, z, n, lo, rows):
        c = coupling[level]
        mid = u[pl.ds(z, n), lo : lo + rows, :]
        total = c[0] * (u[pl.ds(z - 1, n), lo : lo + rows, :] + u[pl.ds(z + 1, n), lo : lo + rows, :])
        total += c[1] * (u[pl.ds(z, n), lo - 1 : lo + rows - 1, :] + u[pl.ds(z, n), lo + 1 : lo + rows + 1, :])
        if level == 0:
            total += left[0] * lane_roll(mid, 1) + right[0] * lane_roll(mid, -1)
        else:
            total += c[2] * (lane_roll(mid, 1) + lane_roll(mid, -1))
        return mid, total

    def over(z0, count, step, body):
        def one_step(i, _):
            body(z0 + i * step)
            return 0

        lax.fori_loop(0, count // step, one_step, 0)

    def sweep(level, u, s, slot, d, z, n, lo, rows):
        mid, total = neighbours(level, u, z, n, lo, rows)
        return (1.0 - OMEGA) * mid + d[pl.ds(z, n), lo : lo + rows, :] * (s[slot, pl.ds(z, n), lo : lo + rows, :] + total)

    def residual(level, u, s, slot, dg, z, n, lo, rows, z_own):
        mid, total = neighbours(level, u, z, n, lo, rows)
        return s[slot, pl.ds(z, n), lo : lo + rows, :] - dg[pl.ds(z - z_own, n)] * mid + total

    def restrict0(fine, slot):
        def body(z):
            a = fine(z)
            i = (z - 4) // 2
            for k in range(2):
                T0[i + k] = a[2 * k] + a[2 * k + 1]

        over(4, 16, 4, body)

        def rows(i):
            e = T0[pl.ds(i, 4), pl.ds(0, 16, stride=2), :] + T0[pl.ds(i, 4), pl.ds(1, 16, stride=2), :]
            S1[slot, pl.ds(5 + i, 4), 16:32, :] = dot(flat(e), Rx[...]).reshape(4, 16, LANES)

        over(0, 8, 4, rows)

    def restrict1(fine, slot):
        a = fine(5)
        for k in range(4):
            T1[k] = a[2 * k] + a[2 * k + 1]
        e = T1[:, pl.ds(0, 8, stride=2), :] + T1[:, pl.ds(1, 8, stride=2), :]
        G[slot, slab] = dot(flat(e), Rx1[...]).reshape(4, 8, LANES)

    def gathered(slot):
        for j in range(4):
            total = G[slot, j] + G[slot, 4 + j] + G[slot, 8 + j] + G[slot, 12 + j]
            S2[:, 8 * j : 8 * j + 8, :] = total

    def restrict2(a):
        T2[0] = a[0] + a[1]
        T2[1] = a[2] + a[3]
        e = T2[:, pl.ds(0, 16, stride=2), :] + T2[:, pl.ds(1, 16, stride=2), :]
        return dot(e[0], R3a[...]) + dot(e[1], R3b[...])

    first_chunk, last_chunk = lane_mask(lane >= 32), lane_mask(lane < 96)

    def neighbours2():
        c = coupling[2]
        mid = U2[:, 8:40, :]
        before = jnp.concatenate([(lane_roll(mid[3], 32) * first_chunk)[None], mid[:3]], axis=0)
        after = jnp.concatenate([mid[1:], (lane_roll(mid[0], -32) * last_chunk)[None]], axis=0)
        total = c[0] * (before + after) + c[1] * (U2[:, 7:39, :] + U2[:, 9:41, :])
        total += left[2] * lane_roll(mid, 1) + right[2] * lane_roll(mid, -1)
        return mid, total

    def sweep2():
        mid, total = neighbours2()
        U2[:, 8:40, :] = (1.0 - OMEGA) * mid + D2[...] * (S2[...] + total)

    row16 = lax.broadcasted_iota(jnp.int32, (16, LANES), 0)
    zeros16, ones16 = jnp.zeros((16, LANES), F32), jnp.ones((16, LANES), F32)
    up3 = jnp.where(row16 > 0, ones16, zeros16) * coupling[3][1]
    down3 = jnp.where(row16 < 15, ones16, zeros16) * coupling[3][1]
    before3 = lane_mask(lane >= 16) * coupling[3][0]
    after3 = lane_mask(lane < 112) * coupling[3][0]

    def level3(s):
        d = D3[...]
        u = d * s
        for _ in range(COARSE_SWEEPS - 1):
            total = before3 * lane_roll(u, 16) + after3 * lane_roll(u, -16)
            total += up3 * pltpu.roll(u, 1, 0) + down3 * pltpu.roll(u, 15, 0)
            total += left[3] * lane_roll(u, 1) + right[3] * lane_roll(u, -1)
            u = (1.0 - OMEGA) * u + d * (s + total)
        return u

    def inside(level, z, n, lo, rows):
        g = GEOMETRY[level]
        zi = lax.broadcasted_iota(jnp.int32, (n, rows, LANES), 0) + (z - g["own_z"] + g["nz"] * cz)
        yi = lax.broadcasted_iota(jnp.int32, (n, rows, LANES), 1) + (lo - g["own_y"] + g["ny"] * cy)
        keep = (zi >= 0) & (zi < 4 * g["nz"]) & (yi >= 0) & (yi < 4 * g["ny"])
        if level:
            keep = keep & (lax.broadcasted_iota(jnp.int32, (n, rows, LANES), 2) < 64)
        return keep

    finish(reaction_moves)
    S0[1, pl.ds(4 + 4 * cy, 4), 16:48, :] = reaction_ref[:, pl.ds(pl.multiple_of(32 * cy, 32), 32), :]
    begin(halo(0, 1))
    restrict0(lambda z: S0[1, pl.ds(z, 4), 16:48, :], 1)
    begin(halo(1, 1))
    restrict1(lambda z: S1[1, pl.ds(z, 8), 16:32, :], 1)
    begin(gather(1))
    VB[pl.ds(4 * cy, 4)] = vol_ref[:, pl.ds(pl.multiple_of(32 * cy, 32), 32), :]

    def diag0(z):
        DG0[pl.ds(z - 4, 4)] = S0[1, pl.ds(z, 4), 16:48, :] + center[0]

    over(4, 16, 4, diag0)
    DG1[...] = S1[1, 5:13, 16:32, :] + center[1]
    finish(halo(0, 1))

    def dinv0(z):
        D0[pl.ds(z, 2), 8:56, :] = jnp.where(
            inside(0, z, 2, 8, 48), OMEGA / (S0[1, pl.ds(z, 2), 8:56, :] + center[0]), jnp.zeros((2, 48, LANES), F32)
        )

    over(1, 22, 2, dinv0)
    finish(halo(1, 1))

    def dinv1(z):
        D1[pl.ds(z, 2), 8:40, :] = jnp.where(
            inside(1, z, 2, 8, 32), OMEGA / (S1[1, pl.ds(z, 2), 8:40, :] + center[1]), jnp.zeros((2, 32, LANES), F32)
        )

    over(1, 16, 2, dinv1)
    finish(gather(1))
    gathered(1)
    DG2[...] = S2[...] + center[2]
    D2[...] = OMEGA / DG2[...]
    D3[...] = OMEGA / (restrict2(S2[...]) + center[3])
    finish(volume_moves)
    finish(weight_moves)
    weight_total = WS[...]
    for d in range(1, 8):
        weight_total += WB[d]
    IW[...] = 1.0 / weight_total

    def vcycle(slot, use):
        def first0(z):
            U0a[pl.ds(z, 2), 8:56, :] = D0[pl.ds(z, 2), 8:56, :] * S0[slot, pl.ds(z, 2), 8:56, :]

        over(1, 22, 2, first0)

        def pre0(z):
            U0b[pl.ds(z, 4), 8:56, :] = sweep(0, U0a, S0, slot, D0, z, 4, 8, 48)

        over(2, 20, 4, pre0)
        restrict0(lambda z: residual(0, U0b, S0, slot, DG0, z, 4, 16, 32, 4), slot)
        begin(halo(1, slot))
        finish(halo(1, slot))

        def first1(z):
            U1a[pl.ds(z, 4), 8:40, :] = D1[pl.ds(z, 4), 8:40, :] * S1[slot, pl.ds(z, 4), 8:40, :]

        over(1, 16, 4, first1)

        def pre1(z):
            U1b[pl.ds(z, 7), 8:40, :] = sweep(1, U1a, S1, slot, D1, z, 7, 8, 32)

        over(2, 14, 7, pre1)
        restrict1(lambda z: residual(1, U1b, S1, slot, DG1, z, 8, 16, 16, 5), slot)
        begin(gather(slot))
        finish(gather(slot))
        gathered(slot)

        U2[:, 8:40, :] = D2[...] * S2[...]
        sweep2()
        mid, total = neighbours2()
        s3 = restrict2(S2[...] - DG2[...] * mid + total)
        u3 = level3(s3)
        for k, matrix_ref in ((0, P3a), (1, P3b)):
            p = dot(u3, matrix_ref[...])
            C2[k, pl.ds(0, 16, stride=2), :] = p
            C2[k, pl.ds(1, 16, stride=2), :] = p
        for k in range(4):
            U2[k, 8:40, :] += C2[k // 2]
        sweep2()
        sweep2()

        near = U2[:, pl.ds(pl.multiple_of(8 * cy, 8), 24), :][:, 4:20, :]
        wide = jnp.concatenate(
            [dot(flat(near[2:4]), PM[...]), dot(flat(near), P0[...]), dot(flat(near[0:2]), PP[...])], axis=0
        ).reshape(8, 16, LANES)
        C1[:, pl.ds(0, 16, stride=2), :] = wide
        C1[:, pl.ds(1, 16, stride=2), :] = wide
        for k in range(8):
            U1b[1 + 2 * k, 8:40, :] += C1[k]
            U1b[2 + 2 * k, 8:40, :] += C1[k]

        def post1a(z):
            U1a[pl.ds(z, 6), 8:40, :] = sweep(1, U1b, S1, slot, D1, z, 6, 8, 32)

        over(3, 12, 6, post1a)

        def post1b(z):
            U1b[pl.ds(z, 5), 8:40, :] = sweep(1, U1a, S1, slot, D1, z, 5, 8, 32)

        over(4, 10, 5, post1b)

        def widen0(i):
            wide = dot(flat(U1b[pl.ds(4 + i, 5), 12:36, :]), Px[...]).reshape(5, 24, LANES)
            C0[:, pl.ds(0, 24, stride=2), :] = wide
            C0[:, pl.ds(1, 24, stride=2), :] = wide
            for k in range(5):
                U0b[2 + 2 * (i + k), 8:56, :] += C0[k]
                U0b[3 + 2 * (i + k), 8:56, :] += C0[k]

        over(0, 10, 5, widen0)

        def post0a(z):
            U0a[pl.ds(z, 3), 8:56, :] = sweep(0, U0b, S0, slot, D0, z, 3, 8, 48)

        over(3, 18, 3, post0a)

        def post0b(z):
            use(z, sweep(0, U0a, S0, slot, D0, z, 4, 16, 32))

        over(4, 16, 4, post0b)

    def centroid():
        sibling = (member + 1 - 2 * mc, slab)
        swap = remote(LB.at[pl.ds(8 * (1 - mc), 8)], XB, x_send, x_recv, sibling)
        swap.start()
        swap.wait()
        HB[...] = LB[pl.ds(8 * mc, 8)] + XB[...]
        pieces = []
        for d in range(1, 4):
            to = lax.rem(mx + d, 4)
            pieces.append(
                remote(HB.at[pl.ds(2 * to, 2)], PB.at[d - 1], p_send.at[d - 1], p_recv.at[d - 1], (2 * to + mc, slab))
            )
        begin(pieces)
        finish(pieces)
        total = HB[pl.ds(2 * mx, 2)] + PB[0] + PB[1] + PB[2]
        inverse = jnp.broadcast_to(IW[...][None, None], (2, 4, 8, LANES)).reshape(2, 32, LANES)
        own = 8 * mc + 2 * mx
        CB[pl.ds(own, 2)] = jnp.exp(total * inverse)
        spread, passed = [], []
        for d in range(1, 4):
            to = lax.rem(mx + d, 4)
            spread.append(
                remote(CB.at[pl.ds(own, 2)], CB.at[pl.ds(own, 2)], c_send.at[d - 1], c_recv.at[d - 1], (2 * to + mc, slab))
            )
        for d in range(4):
            at = 8 * mc + 2 * lax.rem(mx - d + 4, 4)
            passed.append(remote(CB.at[pl.ds(at, 2)], CB.at[pl.ds(at, 2)], f_send.at[d], f_recv.at[d], sibling))
        begin(spread)
        passed[0].start()
        for d in range(1, 4):
            spread[d - 1].wait_recv()
            passed[d].start()
        for c in spread:
            c.wait_send()
        finish(passed)

    def half_step(n, _):
        slot = lax.rem(n, 2)

        @pl.when(n > 0)
        def _():
            finish(halo(0, slot))

        def keep(z, h):
            MB[pl.ds(z - 4, 4)] = h

        vcycle(slot, keep)

        @pl.when(slot == 0)
        def _():
            def partner(z):
                S0[1, pl.ds(z, 4), 16:48, :] = VB[pl.ds(z - 4, 4)] / MB[pl.ds(z - 4, 4)]

            over(4, 16, 4, partner)

        @pl.when(slot == 1)
        def _():
            def marginal(z):
                m = S0[0, pl.ds(z, 4), 16:48, :] * MB[pl.ds(z - 4, 4)]
                MB[pl.ds(z - 4, 4)] = m
                LB[pl.ds(z - 4, 4)] = weight_ref[0] * jnp.log(m)

            over(4, 16, 4, marginal)
            centroid()

            def update(z):
                S0[0, pl.ds(z, 4), 16:48, :] = S0[0, pl.ds(z, 4), 16:48, :] * CB[pl.ds(z - 4, 4)] / MB[pl.ds(z - 4, 4)]

            over(4, 16, 4, update)

        @pl.when(n < 2 * ITERS - 1)
        def _():
            begin(halo(0, 1 - slot))

        return 0

    lax.fori_loop(0, 2 * ITERS, half_step, 0)

    moves = to_slabs(CB, 0, 0, cent_out, o_send.at[0], o_recv.at[0]) + to_slabs(
        S0.at[0], 4, 16, mult_out, o_send.at[1], o_recv.at[1]
    )
    begin(moves)
    mine = pl.ds(pl.multiple_of(32 * cy, 32), 32)
    cent_out[:, mine, :] = CB[pl.ds(4 * cy, 4)]
    mult_out[:, mine, :] = S0[0, pl.ds(4 + 4 * cy, 4), 16:48, :]
    finish(moves)


def body(nonnegative_volumes, reaction, diffusivity, member_weights):
    vmem, smem = pl.BlockSpec(memory_space=pltpu.VMEM), pl.BlockSpec(memory_space=pltpu.SMEM)
    field = jax.ShapeDtypeStruct((4, 128, 128), F32)

    def buffer(*shape):
        return pltpu.VMEM((*shape, LANES), F32)

    dma = pltpu.SemaphoreType.DMA
    scratch = [
        buffer(2, 24, 64), buffer(24, 64), buffer(16, 32), buffer(24, 64), buffer(24, 64), buffer(5, 48), buffer(8, 32),
        buffer(2, 18, 48), buffer(18, 48), buffer(8, 16), buffer(18, 48), buffer(18, 48), buffer(8, 32), buffer(4, 16),
        buffer(2, 16, 4, 8), buffer(4, 32), buffer(4, 32), buffer(4, 32), buffer(4, 48), buffer(2, 32), buffer(2, 32), buffer(16),
        buffer(16, 32), buffer(16, 32), buffer(16, 32), buffer(8, 32), buffer(8, 32), buffer(3, 2, 32), buffer(16, 32),
        buffer(8), buffer(8, 8), buffer(8),
        *[buffer(128) for _ in range(10)],
        dma((2, 8)), dma((2, 8)), dma((2, 8)), dma((2, 8)), dma((2, 16)), dma((2, 16)),
        dma((3,)), dma((3,)), dma((3,)), dma((3,)), dma((7,)), dma((7,)),
        dma, dma, dma((3,)), dma((3,)), dma((3,)), dma((3,)), dma((4,)), dma((4,)), dma((2, 3)), dma((2, 3)),
    ]
    centroid, multipliers = pl.pallas_call(
        kernel,
        out_shape=(field, field),
        in_specs=[vmem, vmem, smem, smem],
        out_specs=(vmem, vmem),
        scratch_shapes=scratch,
        compiler_params=pltpu.CompilerParams(collective_id=0, has_side_effects=True, vmem_limit_bytes=40 * 2**20),
    )(nonnegative_volumes[0], reaction, diffusivity, member_weights)
    return centroid, multipliers[None]


def solution(mesh):
    return jax.shard_map(
        body,
        mesh=mesh,
        in_specs=(P("member", "slab", None, None), P("slab", None, None), P(), P("member")),
        out_specs=(P("slab", None, None), P("member", "slab", None, None)),
        check_vma=False,
    )
```

time: 1280 us -> 198 us (0.15); the launches traced: 1260 us -> 198 us
  waiting for transfers between devices: 294 us -> 0 us
  starting transfers between devices: 286 us -> 0 us
  other arithmetic: 249 us -> 0 us
  blocking collectives: 240 us -> 0 us
  Pallas kernels: 0 us -> 193 us
  local copies, waits for them, and re-layouts: 165 us -> 3.95 us
  between operations: 25.4 us -> 1.3 us
    ppermute x96 -> x0, starting transfers between devices: 286 us -> none  [the longest x48 224 us: with_halo(): lax.ppermute(tail, axis, [(i, (i + 1) % count) for i in range(ends)])]
    psum x3 -> x0, waiting for transfers between devices: 244 us -> none  [body(): log_total = lax.psum(weighted_log, 'member')]
    all_gather x7 -> x0, blocking collectives: 194 us -> none  [the longest x6 168 us: vcycle(): coarsened_grid = lax.all_gather(coarsened_grid, 'slab', axis=0, tiled=True)]
    pallas_call x0 -> x1, Pallas kernels: none -> 193 us  [body(): pl.pallas_call(kernel, out_shape=(field, field), in_specs=[vmem, vmem, sm...]
    add x151 -> x0, other arithmetic: 183 us -> none  [the longest x84 172 us: vcycle(): iterate + OMEGA * (source - apply_operator(iterate, multigrid_depth, reac...]
    reshape x12 -> x0, local copies, waits for them, and re-layouts: 97.6 us -> none  [prolong(): return spread.reshape(2 * zdim, 2 * ydim, 2 * xdim)]
    broadcast_in_dim x30 -> x0, local copies, waits for them, and re-layouts: 59 us -> none  [prolong(): jnp.broadcast_to(array[:, None, :, None, :, None], (zdim, 2, ydim, 2, xdi...]
    ppermute x96 -> x0, waiting for transfers between devices: 50.6 us -> none  [the longest x48 50.5 us: with_halo(): lax.ppermute(tail, axis, [(i, (i + 1) % count) for i in range(ends)])]
  transfers between devices with their start and end apart: 99 -> 0, of which waited for: 48 -> 0; matrix products, arithmetic and copies ran while one was open for 0% -> 0% of each run, Pallas kernels for 0% -> 0%
where the time goes in v1:
time: 198 us
  Pallas kernels  193 us (97%)
  local copies, waits for them, and re-layouts  3.95 us (2%)
    pallas_call x1, Pallas kernels, body(): pl.pallas_call(kernel, out_shape=(field, field), in_specs=[vmem, vmem, sm...  193 us

profile of v1, /device:TPU:1, one launch (start us, length us, event | category | flops | bytes accessed | tf_op | source)
XLA Modules:
  0.0 198.1 jit_solution(13506873681530141420)
XLA Ops:
  1.3 0.0 copy-start.2
  1.3 0.6 copy-done.2
  1.9 0.0 copy-start
  1.9 0.9 copy-done
  2.9 0.0 copy-start.1
  2.9 0.9 copy-done.1
  3.8 192.9 %shard_map.59 = (f32[4,128,128]{2,1,0:T(8,128)S(1)}, f32[4,128,128]{2,1,0:T(8,128)S(1)}) custom-call(f32[4,128,128]{2,1,0:T(8,128)S(1)} %bitcast.2, f32[4,128,128]{2,1,0:T(8,128)S(1)} %copy-done.1, f32[3]{0:T(128)S(1)} %copy-done.2, f32[1]{0:T(128)S(6)} %copy.8.weight_ref), custom_call_target="tpu_custom_call" | custom-call | tf_op jit(solution)/shard_map/pallas_call | solution.py:508
  196.7 0.7 copy.9
  197.4 0.7 copy.10
Async XLA Ops:
  1.3 0.7 copy-start.2
  1.9 0.9 copy-start
  2.9 0.9 copy-start.1

commit v2 on v1

v2 whole, which is shorter than its diff:
```python
import jax
import jax.numpy as jnp
from jax import lax
from jax.experimental import pallas as pl
from jax.experimental.pallas import tpu as pltpu
from jax.sharding import PartitionSpec as P

ITERS = 3
COARSE_SWEEPS = 8
OMEGA = 0.8
LANES = 128
NZ, NY = 64, 128
F32 = jnp.float32
MESH = pl.DeviceIdType.MESH
DIRECTIONS = ((-1, 0), (1, 0), (0, -1), (0, 1), (-1, -1), (-1, 1), (1, -1), (1, 1))

GEOMETRY = (dict(own_z=4, own_y=16, nz=16, ny=32), dict(own_z=5, own_y=12, nz=8, ny=16))


def dot(a, b):
    return jnp.dot(a, b, precision=lax.Precision.HIGHEST, preferred_element_type=F32)


def flat(a):
    return a.reshape(-1, LANES)


def lane_roll(a, shift):
    return pltpu.roll(flat(a), shift % LANES, 1).reshape(a.shape)


def kernel(
    vol_ref, reaction_ref, diff_ref, weight_ref, cent_out, mult_out,
    S0, SC, D0, DG0, UA, UB, U0a, U0b, C0, T0,
    S1, S1C, D1, DG1, VA, VC, U1a, U1b, C1, T1, LZ, LY, LD,
    G, S2, D2, DG2, U2, T2, C2, D3,
    VB, MB, LB, XB, HB, PB, CB, WS, WB, IW,
    Rx, Rx1, R3, P3, E1, Px,
    h0_send, h0_recv, h1_send, h1_recv, g_send, g_recv,
    ra_send, ra_recv, va_send, va_recv, w_send, w_recv,
    x_send, x_recv, p_send, p_recv, c_send, c_recv, f_send, f_recv, o_send, o_recv,
):
    member, slab = lax.axis_index("member"), lax.axis_index("slab")
    cz, cy = slab // 4, lax.rem(slab, 4)
    mx, mc = member // 2, lax.rem(member, 2)

    def at_slab(dz, dy):
        return lax.rem(cz + dz + 4, 4) * 4 + lax.rem(cy + dy + 4, 4)

    def remote(src, dst, send, recv, to):
        return pltpu.make_async_remote_copy(
            src_ref=src, dst_ref=dst, send_sem=send, recv_sem=recv, device_id=to, device_id_type=MESH
        )

    for ref in (SC, UA, UB, VA, VC, S1C, U0a, U0b, U1a, U1b, U2, LZ, LY, LD, T1):
        ref[...] = jnp.zeros(ref.shape, F32)
    S0[...] = jnp.ones(S0.shape, F32)

    barrier = pltpu.get_barrier_semaphore()
    for d in range(1, 16):
        pl.semaphore_signal(barrier, inc=1, device_id=(member, at_slab(d // 4, d % 4)), device_id_type=MESH)
    for d in range(1, 8):
        pl.semaphore_signal(barrier, inc=1, device_id=(lax.rem(member + d, 8), slab), device_id_type=MESH)
    pl.semaphore_wait(barrier, 22)

    def inner(dz, dy):
        return (cz + dz >= 0) & (cz + dz < 4) & (cy + dy >= 0) & (cy + dy < 4)

    def halo0(slot):
        copies = []
        for k, (dz, dy) in enumerate(DIRECTIONS):
            zs, zn, zd = {-1: (4, 3, 20), 0: (4, 16, 4), 1: (17, 3, 1)}[dz]
            ys, yn, yd = {-1: (16, 8, 48), 0: (16, 32, 16), 1: (40, 8, 8)}[dy]
            copies.append((
                dz, dy,
                remote(
                    S0.at[slot, pl.ds(zs, zn), pl.ds(ys, yn)], S0.at[slot, pl.ds(zd, zn), pl.ds(yd, yn)],
                    h0_send.at[slot, k], h0_recv.at[slot, k], (member, at_slab(dz, dy)),
                ),
            ))
        return copies

    def landing1(k, slot):
        if k < 2:
            return LZ.at[slot, k]
        return LY.at[slot, k - 2] if k < 4 else LD.at[slot, k - 4]

    def halo1(slot):
        copies = []
        for k, (dz, dy) in enumerate(DIRECTIONS):
            z = {-1: pl.ds(4, 5), 0: pl.ds(4, 10), 1: pl.ds(9, 5)}[dz]
            y = {-1: pl.ds(8, 8), 0: pl.ds(8, 24), 1: pl.ds(24, 8)}[dy]
            copies.append((
                dz, dy,
                remote(
                    S1C.at[z, y], landing1(k, slot),
                    h1_send.at[slot, k], h1_recv.at[slot, k], (member, at_slab(dz, dy)),
                ),
            ))
        return copies

    def begin_near(copies):
        for dz, dy, c in copies:
            pl.when(inner(dz, dy))(c.start)

    def finish_near(copies):
        for dz, dy, c in copies:
            pl.when(inner(-dz, -dy))(c.wait_recv)
        for dz, dy, c in copies:
            pl.when(inner(dz, dy))(c.wait_send)

    def gather(slot):
        return [
            remote(
                G.at[slot, slab], G.at[slot, slab],
                g_send.at[slot, d], g_recv.at[slot, d], (member, at_slab(d // 4, d % 4)),
            )
            for d in range(1, 16)
        ]

    def begin(copies):
        for c in copies:
            c.start()

    def finish(copies):
        for c in copies:
            c.wait()

    def to_blocks(src, dst, dst_z, dst_y, send, recv):
        copies = []
        for d in range(1, 4):
            to = lax.rem(cy + d, 4)
            copies.append(
                remote(
                    src.at[:, pl.ds(pl.multiple_of(32 * to, 32), 32)],
                    dst.at[pl.ds(dst_z + 4 * cy, 4), pl.ds(dst_y, 32)],
                    send.at[d - 1], recv.at[d - 1], (member, cz * 4 + to),
                )
            )
        return copies

    def to_slabs(src, src_z, src_y, dst, send, recv):
        copies = []
        for d in range(1, 4):
            to = lax.rem(cy + d, 4)
            copies.append(
                remote(
                    src.at[pl.ds(src_z + 4 * to, 4), pl.ds(src_y, 32)],
                    dst.at[:, pl.ds(pl.multiple_of(32 * cy, 32), 32)],
                    send.at[d - 1], recv.at[d - 1], (member, cz * 4 + to),
                )
            )
        return copies

    reaction_moves = to_blocks(reaction_ref, S0.at[1], 4, 16, ra_send, ra_recv)
    volume_moves = to_blocks(vol_ref, VB, 0, 0, va_send, va_recv)
    begin(reaction_moves)
    begin(volume_moves)
    WS[...] = jnp.full((8, LANES), weight_ref[0], F32)
    weight_moves = [
        remote(WS, WB.at[d], w_send.at[d - 1], w_recv.at[d - 1], (lax.rem(member + d, 8), slab)) for d in range(1, 8)
    ]
    begin(weight_moves)

    coupling = [[diff_ref[i] * (0.25**level) for i in range(3)] for level in range(4)]
    center = [2.0 * (c[0] + c[1] + c[2]) for c in coupling]

    lane = lax.broadcasted_iota(jnp.int32, (1, LANES), 1)
    one, zero = jnp.ones((1, LANES), F32), jnp.zeros((1, LANES), F32)

    def lane_mask(keep):
        return jnp.where(keep, one, zero)

    row_i = lax.broadcasted_iota(jnp.int32, (LANES, LANES), 0)
    col_i = lax.broadcasted_iota(jnp.int32, (LANES, LANES), 1)

    def half(a):
        return lax.shift_right_logical(a, 1)

    def matrix(keep, value=1.0):
        return jnp.where(keep, jnp.full((LANES, LANES), value, F32), jnp.zeros((LANES, LANES), F32))

    Rx[...] = matrix(half(row_i) == col_i, 0.125)
    Px[...] = matrix(row_i == half(col_i))
    for q in range(4):
        block = slice(LANES * q, LANES * q + LANES)
        Rx1[block, :] = matrix((row_i < 64) & (half(row_i) + 32 * q == col_i), 0.125)
        E1[:, block] = matrix((col_i < 64) & (row_i == half(col_i) + 32 * q))
        R3[block, :] = matrix(16 * (2 * q + lax.shift_right_logical(row_i, 6)) + half(row_i & 31) == col_i, 0.125)
        P3[:, block] = matrix(16 * (2 * q + lax.shift_right_logical(col_i, 6)) + half(col_i & 31) == row_i)

    left = [lane_mask(lane > 0) * coupling[0][2], None, lane_mask((lane & 31) > 0) * coupling[2][2], lane_mask((lane & 15) > 0) * coupling[3][2]]
    right = [lane_mask(lane < 127) * coupling[0][2], None, lane_mask((lane & 31) < 31) * coupling[2][2], lane_mask((lane & 15) < 15) * coupling[3][2]]

    def neighbours(level, u, z, n, lo, rows):
        c = coupling[level]
        mid = u[pl.ds(z, n), lo : lo + rows, :]
        total = c[0] * (u[pl.ds(z - 1, n), lo : lo + rows, :] + u[pl.ds(z + 1, n), lo : lo + rows, :])
        total += c[1] * (u[pl.ds(z, n), lo - 1 : lo + rows - 1, :] + u[pl.ds(z, n), lo + 1 : lo + rows + 1, :])
        if level == 0:
            total += left[0] * lane_roll(mid, 1) + right[0] * lane_roll(mid, -1)
        else:
            total += c[2] * (lane_roll(mid, 1) + lane_roll(mid, -1))
        return mid, total

    def over(z0, count, step, body):
        def one_step(i, _):
            body(z0 + i * step)
            return 0

        lax.fori_loop(0, count // step, one_step, 0)

    def sweep(level, u, s, d, z, n, lo, rows):
        mid, total = neighbours(level, u, z, n, lo, rows)
        return (1.0 - OMEGA) * mid + d[pl.ds(z, n), lo : lo + rows, :] * (s[pl.ds(z, n), lo : lo + rows, :] + total)

    def residual(level, u, s, dg, z, n, lo, rows):
        mid, total = neighbours(level, u, z, n, lo, rows)
        return s[pl.ds(z, n), lo : lo + rows, :] - dg[pl.ds(z, n), lo : lo + rows, :] * mid + total

    def restrict0(fine):
        def body(z):
            a = fine(z)
            for k in range(2):
                T0[(z - 2) // 2 + k] = a[2 * k] + a[2 * k + 1]

        over(2, 20, 4, body)

        def rows(i):
            e = T0[pl.ds(i, 5), pl.ds(0, 24, stride=2), :] + T0[pl.ds(i, 5), pl.ds(1, 24, stride=2), :]
            S1C[pl.ds(4 + i, 5), 8:32, :] = dot(flat(e), Rx[...]).reshape(5, 24, LANES)

        over(0, 10, 5, rows)

    def restrict1(fine, slot):
        def body(z):
            a = fine(z)
            for k in range(4):
                T1[(z - 1) // 2 + k, 4:28, :] = a[2 * k] + a[2 * k + 1]

        over(1, 16, 8, body)
        e = T1[:, pl.ds(0, 16, stride=2), :] + T1[:, pl.ds(1, 16, stride=2), :]
        own = jnp.concatenate([e[2], e[3], e[4], e[5]], axis=1)
        sides = jnp.concatenate([e[6], e[7], e[0], e[1]], axis=1)
        m = dot(jnp.concatenate([own, sides], axis=0), Rx1[...]).reshape(2, 16, LANES)
        G[slot, slab, :, 0:8, :] = m[:, 4:12]
        G[slot, slab, :, 8:12, :] = m[:, 12:16]
        G[slot, slab, :, 12:16, :] = m[:, 0:4]

    upper_half, upper_rows = lane >= 64, lax.broadcasted_iota(jnp.int32, (8, LANES), 0) < 4
    nothing = jnp.zeros((8, LANES), F32)

    def gathered(slot):
        def rows(c, j, g):
            below = G[slot, 4 * c + j - 1, g, 8:16, :] if j > 0 else nothing
            above = G[slot, 4 * c + j + 1, g, 8:16, :] if j < 3 else nothing
            return G[slot, 4 * c + j, g, 0:8, :] + jnp.where(upper_rows, below, above)

        for j in range(4):
            side = [nothing] + [rows(c, j, 1) for c in range(4)] + [nothing]
            for c in range(4):
                S2[c, 8 * j : 8 * j + 8, :] = rows(c, j, 0) + jnp.where(upper_half, side[c + 2], side[c])

    def restrict2(a):
        T2[...] = a
        e = T2[:, pl.ds(0, 16, stride=2), :] + T2[:, pl.ds(1, 16, stride=2), :]
        return dot(jnp.concatenate([e[0], e[1], e[2], e[3]], axis=1), R3[...])

    first_chunk, last_chunk = lane < 32, lane >= 96
    plane2 = jnp.zeros((1, 32, LANES), F32)

    def neighbours2():
        c = coupling[2]
        mid = U2[1:5, 8:40, :]
        up, down = lane_roll(mid, 32), lane_roll(mid, -32)
        before = jnp.where(first_chunk, jnp.concatenate([plane2, up[:3]], axis=0), up)
        after = jnp.where(last_chunk, jnp.concatenate([down[1:], plane2], axis=0), down)
        total = c[0] * (before + after) + c[1] * (U2[1:5, 7:39, :] + U2[1:5, 9:41, :])
        total += left[2] * lane_roll(mid, 1) + right[2] * lane_roll(mid, -1)
        return mid, total

    def sweep2():
        mid, total = neighbours2()
        U2[1:5, 8:40, :] = (1.0 - OMEGA) * mid + D2[...] * (S2[...] + total)

    row16 = lax.broadcasted_iota(jnp.int32, (16, LANES), 0)
    zeros16, ones16 = jnp.zeros((16, LANES), F32), jnp.ones((16, LANES), F32)
    up3 = jnp.where(row16 > 0, ones16, zeros16) * coupling[3][1]
    down3 = jnp.where(row16 < 15, ones16, zeros16) * coupling[3][1]
    before3 = lane_mask(lane >= 16) * coupling[3][0]
    after3 = lane_mask(lane < 112) * coupling[3][0]

    def level3(s):
        d = D3[...]
        u = d * s
        for _ in range(COARSE_SWEEPS - 1):
            total = before3 * lane_roll(u, 16) + after3 * lane_roll(u, -16)
            total += up3 * pltpu.roll(u, 1, 0) + down3 * pltpu.roll(u, 15, 0)
            total += left[3] * lane_roll(u, 1) + right[3] * lane_roll(u, -1)
            u = (1.0 - OMEGA) * u + d * (s + total)
        return u

    def inside(level, z, n, lo, rows):
        g = GEOMETRY[level]
        zi = lax.broadcasted_iota(jnp.int32, (n, rows, LANES), 0) + (z - g["own_z"] + g["nz"] * cz)
        yi = lax.broadcasted_iota(jnp.int32, (n, rows, LANES), 1) + (lo - g["own_y"] + g["ny"] * cy)
        keep = (zi >= 0) & (zi < 4 * g["nz"]) & (yi >= 0) & (yi < 4 * g["ny"])
        if level:
            keep = keep & (lax.broadcasted_iota(jnp.int32, (n, rows, LANES), 2) < 64)
        return keep

    finish(reaction_moves)
    mine = pl.ds(pl.multiple_of(32 * cy, 32), 32)
    S0[1, pl.ds(4 + 4 * cy, 4), 16:48, :] = reaction_ref[:, mine, :]
    begin_near(halo0(1))
    SC[4:20, 16:48, :] = S0[1, 4:20, 16:48, :]
    restrict0(lambda z: SC[pl.ds(z, 4), 8:56, :])
    restrict1(lambda z: S1C[pl.ds(z, 8), 8:32, :], 1)
    begin(gather(1))
    begin_near(halo1(1))
    VB[pl.ds(4 * cy, 4)] = vol_ref[:, mine, :]

    def summed1(slot):
        finish_near(halo1(slot))
        S1[1:17, 8:32, :] = S1C[1:17, 8:32, :]
        for k, (dz, dy) in enumerate(DIRECTIONS):
            z = {-1: slice(12, 17), 0: slice(4, 14), 1: slice(1, 6)}[dz]
            y = {-1: slice(24, 32), 0: slice(8, 32), 1: slice(8, 16)}[dy]
            S1[z, y, :] += landing1(k, slot)[...]

    finish_near(halo0(1))

    def diag0(z):
        diag = S0[1, pl.ds(z, 2), 8:56, :] + center[0]
        DG0[pl.ds(z, 2), 8:56, :] = diag
        D0[pl.ds(z, 2), 8:56, :] = jnp.where(inside(0, z, 2, 8, 48), OMEGA / diag, jnp.zeros((2, 48, LANES), F32))

    over(1, 22, 2, diag0)
    summed1(1)

    def diag1(z):
        diag = S1[pl.ds(z, 2), 8:32, :] + center[1]
        DG1[pl.ds(z, 2), 8:32, :] = diag
        D1[pl.ds(z, 2), 8:32, :] = jnp.where(inside(1, z, 2, 8, 24), OMEGA / diag, jnp.zeros((2, 24, LANES), F32))

    over(1, 16, 2, diag1)
    finish(gather(1))
    gathered(1)
    DG2[...] = S2[...] + center[2]
    D2[...] = OMEGA / DG2[...]
    D3[...] = OMEGA / (restrict2(S2[...]) + center[3])
    SC[4:20, 16:48, :] = jnp.ones((16, 32, LANES), F32)
    finish(volume_moves)
    finish(weight_moves)
    weight_total = WS[...]
    for d in range(1, 8):
        weight_total += WB[d]
    IW[...] = 1.0 / weight_total

    def vcycle(n, slot, use):
        UA[4:20, 16:48, :] = D0[4:20, 16:48, :] * SC[4:20, 16:48, :]

        def own0(z):
            UB[pl.ds(z, 3), 8:56, :] = sweep(0, UA, SC, D0, z, 3, 8, 48)

        over(3, 18, 3, own0)
        restrict0(lambda z: residual(0, UB, SC, DG0, z, 4, 8, 48))
        VA[4:14, 8:32, :] = D1[4:14, 8:32, :] * S1C[4:14, 8:32, :]

        def own1(z):
            VC[pl.ds(z, 6), 8:32, :] = sweep(1, VA, S1C, D1, z, 6, 8, 24)

        over(3, 12, 6, own1)
        restrict1(lambda z: residual(1, VC, S1C, DG1, z, 8, 8, 24), slot)
        begin(gather(slot))
        begin_near(halo1(slot))

        @pl.when(n > 0)
        def _():
            finish_near(halo0(slot))

        source0 = S0.at[slot]

        def first0(z):
            U0a[pl.ds(z, 2), 8:56, :] = D0[pl.ds(z, 2), 8:56, :] * source0[pl.ds(z, 2), 8:56, :]

        over(1, 22, 2, first0)

        def pre0(z):
            U0b[pl.ds(z, 4), 8:56, :] = sweep(0, U0a, source0, D0, z, 4, 8, 48)

        over(2, 20, 4, pre0)
        summed1(slot)
        U1a[1:17, 8:32, :] = D1[1:17, 8:32, :] * S1[1:17, 8:32, :]

        def pre1(z):
            U1b[pl.ds(z, 7), 8:32, :] = sweep(1, U1a, S1, D1, z, 7, 8, 24)

        over(2, 14, 7, pre1)

        finish(gather(slot))
        gathered(slot)
        U2[1:5, 8:40, :] = D2[...] * S2[...]
        sweep2()
        mid, total = neighbours2()
        u3 = level3(restrict2(S2[...] - DG2[...] * mid + total))
        p = dot(u3, P3[...])
        for k in range(4):
            C2[k, pl.ds(0, 16, stride=2), :] = p[:, LANES * k : LANES * k + LANES]
            C2[k, pl.ds(1, 16, stride=2), :] = p[:, LANES * k : LANES * k + LANES]
        U2[1:5, 8:40, :] += C2[...]
        sweep2()
        sweep2()

        window = pl.ds(pl.multiple_of(8 * cy, 8), 24)
        own = U2[1 + cz, window, :][4:20]
        sides = jnp.where(upper_half, U2[cz, window, :][4:20], U2[2 + cz, window, :][4:20])
        wide = dot(jnp.concatenate([own, sides], axis=0), E1[...])
        for k in range(8):
            r, q = (0, k - 2) if 2 <= k < 6 else (16, (k - 2) % 4)
            C1[k, pl.ds(0, 16, stride=2), :] = wide[r : r + 16, LANES * q : LANES * q + LANES]
            C1[k, pl.ds(1, 16, stride=2), :] = wide[r : r + 16, LANES * q : LANES * q + LANES]
        for k in range(8):
            U1b[1 + 2 * k, 8:32, :] += C1[k, 4:28, :]
            U1b[2 + 2 * k, 8:32, :] += C1[k, 4:28, :]

        def post1a(z):
            U1a[pl.ds(z, 6), 8:32, :] = sweep(1, U1b, S1, D1, z, 6, 8, 24)

        over(3, 12, 6, post1a)

        def post1b(z):
            U1b[pl.ds(z, 5), 8:32, :] = sweep(1, U1a, S1, D1, z, 5, 8, 24)

        over(4, 10, 5, post1b)

        def widen0(i):
            wide = dot(flat(U1b[pl.ds(4 + i, 5), 8:32, :]), Px[...]).reshape(5, 24, LANES)
            C0[:, pl.ds(0, 24, stride=2), :] = wide
            C0[:, pl.ds(1, 24, stride=2), :] = wide
            for k in range(5):
                U0b[2 + 2 * (i + k), 8:56, :] += C0[k]
                U0b[3 + 2 * (i + k), 8:56, :] += C0[k]

        over(0, 10, 5, widen0)

        def post0a(z):
            U0a[pl.ds(z, 3), 8:56, :] = sweep(0, U0b, source0, D0, z, 3, 8, 48)

        over(3, 18, 3, post0a)

        def post0b(z):
            use(z, sweep(0, U0a, source0, D0, z, 4, 16, 32))

        over(4, 16, 4, post0b)

    def centroid():
        sibling = (member + 1 - 2 * mc, slab)
        swap = remote(LB.at[pl.ds(8 * (1 - mc), 8)], XB, x_send, x_recv, sibling)
        swap.start()
        swap.wait()
        HB[...] = LB[pl.ds(8 * mc, 8)] + XB[...]
        pieces = []
        for d in range(1, 4):
            to = lax.rem(mx + d, 4)
            pieces.append(
                remote(HB.at[pl.ds(2 * to, 2)], PB.at[d - 1], p_send.at[d - 1], p_recv.at[d - 1], (2 * to + mc, slab))
            )
        begin(pieces)
        finish(pieces)
        total = HB[pl.ds(2 * mx, 2)] + PB[0] + PB[1] + PB[2]
        inverse = jnp.broadcast_to(IW[...][None, None], (2, 4, 8, LANES)).reshape(2, 32, LANES)
        own = 8 * mc + 2 * mx
        CB[pl.ds(own, 2)] = jnp.exp(total * inverse)
        spread, passed = [], []
        for d in range(1, 4):
            to = lax.rem(mx + d, 4)
            spread.append(
                remote(CB.at[pl.ds(own, 2)], CB.at[pl.ds(own, 2)], c_send.at[d - 1], c_recv.at[d - 1], (2 * to + mc, slab))
            )
        for d in range(4):
            at = 8 * mc + 2 * lax.rem(mx - d + 4, 4)
            passed.append(remote(CB.at[pl.ds(at, 2)], CB.at[pl.ds(at, 2)], f_send.at[d], f_recv.at[d], sibling))
        begin(spread)
        passed[0].start()
        for d in range(1, 4):
            spread[d - 1].wait_recv()
            passed[d].start()
        for c in spread:
            c.wait_send()
        finish(passed)

    def half_step(n, _):
        slot = lax.rem(n, 2)

        def keep(z, h):
            MB[pl.ds(z - 4, 4)] = h

        vcycle(n, slot, keep)

        @pl.when(slot == 0)
        def _():
            def partner(z):
                p = VB[pl.ds(z - 4, 4)] / MB[pl.ds(z - 4, 4)]
                S0[1, pl.ds(z, 4), 16:48, :] = p
                SC[pl.ds(z, 4), 16:48, :] = p

            over(4, 16, 4, partner)

        @pl.when(slot == 1)
        def _():
            def marginal(z):
                m = S0[0, pl.ds(z, 4), 16:48, :] * MB[pl.ds(z - 4, 4)]
                MB[pl.ds(z - 4, 4)] = m
                LB[pl.ds(z - 4, 4)] = weight_ref[0] * jnp.log(m)

            over(4, 16, 4, marginal)
            centroid()

            def update(z):
                p = S0[0, pl.ds(z, 4), 16:48, :] * CB[pl.ds(z - 4, 4)] / MB[pl.ds(z - 4, 4)]
                S0[0, pl.ds(z, 4), 16:48, :] = p
                SC[pl.ds(z, 4), 16:48, :] = p

            over(4, 16, 4, update)

        @pl.when(n < 2 * ITERS - 1)
        def _():
            begin_near(halo0(1 - slot))

        return 0

    lax.fori_loop(0, 2 * ITERS, half_step, 0)

    moves = to_slabs(CB, 0, 0, cent_out, o_send.at[0], o_recv.at[0]) + to_slabs(
        S0.at[0], 4, 16, mult_out, o_send.at[1], o_recv.at[1]
    )
    begin(moves)
    cent_out[:, mine, :] = CB[pl.ds(4 * cy, 4)]
    mult_out[:, mine, :] = S0[0, pl.ds(4 + 4 * cy, 4), 16:48, :]
    finish(moves)


def body(nonnegative_volumes, reaction, diffusivity, member_weights):
    vmem, smem = pl.BlockSpec(memory_space=pltpu.VMEM), pl.BlockSpec(memory_space=pltpu.SMEM)
    field = jax.ShapeDtypeStruct((4, 128, 128), F32)

    def buffer(*shape):
        return pltpu.VMEM((*shape, LANES), F32)

    dma = pltpu.SemaphoreType.DMA
    scratch = [
        buffer(2, 24, 64), *[buffer(24, 64) for _ in range(7)], buffer(5, 48), buffer(10, 48),
        *[buffer(18, 40) for _ in range(8)], buffer(8, 32), buffer(8, 32), buffer(2, 2, 5, 24), buffer(2, 2, 10, 8), buffer(2, 4, 5, 8),
        buffer(2, 16, 2, 16), buffer(4, 32), buffer(4, 32), buffer(4, 32), buffer(6, 48), buffer(4, 32), buffer(4, 32), buffer(16),
        buffer(16, 32), buffer(16, 32), buffer(16, 32), buffer(8, 32), buffer(8, 32), buffer(3, 2, 32), buffer(16, 32),
        buffer(8), buffer(8, 8), buffer(8),
        buffer(128), buffer(512), buffer(512), pltpu.VMEM((128, 512), F32), pltpu.VMEM((128, 512), F32), buffer(128),
        dma((2, 8)), dma((2, 8)), dma((2, 8)), dma((2, 8)), dma((2, 16)), dma((2, 16)),
        dma((3,)), dma((3,)), dma((3,)), dma((3,)), dma((7,)), dma((7,)),
        dma, dma, dma((3,)), dma((3,)), dma((3,)), dma((3,)), dma((4,)), dma((4,)), dma((2, 3)), dma((2, 3)),
    ]
    centroid, multipliers = pl.pallas_call(
        kernel,
        out_shape=(field, field),
        in_specs=[vmem, vmem, smem, smem],
        out_specs=(vmem, vmem),
        scratch_shapes=scratch,
        compiler_params=pltpu.CompilerParams(collective_id=0, has_side_effects=True, vmem_limit_bytes=40 * 2**20),
    )(nonnegative_volumes[0], reaction, diffusivity, member_weights)
    return centroid, multipliers[None]


def solution(mesh):
    return jax.shard_map(
        body,
        mesh=mesh,
        in_specs=(P("member", "slab", None, None), P("slab", None, None), P(), P("member")),
        out_specs=(P("slab", None, None), P("member", "slab", None, None)),
        check_vma=False,
    )
```

time: 198 us -> 153 us (0.77)
  Pallas kernels: 193 us -> 147 us
    pallas_call x1, Pallas kernels: 193 us -> 147 us  [body(): pl.pallas_call(kernel, out_shape=(field, field), in_specs=[vmem, vmem, sm...]
where the time goes in v2:
time: 153 us; the launch traced here: 152 us
  Pallas kernels  147 us (96%)
  local copies, waits for them, and re-layouts  3.95 us (3%)
    pallas_call x1, Pallas kernels, body(): pl.pallas_call(kernel, out_shape=(field, field), in_specs=[vmem, vmem, sm...  147 us
    unnamed x8, local copies, waits for them, and re-layouts  3.95 us

profile of v2, /device:TPU:1, one launch (start us, length us, event | category | flops | bytes accessed | tf_op | source)
XLA Modules:
  0.0 152.3 jit_solution(2788791852557418885)
XLA Ops:
  1.3 0.0 copy-start.2
  1.3 0.6 copy-done.2
  1.9 0.0 copy-start
  1.9 0.9 copy-done
  2.9 0.0 copy-start.1
  2.9 0.9 copy-done.1
  3.8 147.1 %shard_map.59 = (f32[4,128,128]{2,1,0:T(8,128)S(1)}, f32[4,128,128]{2,1,0:T(8,128)S(1)}) custom-call(f32[4,128,128]{2,1,0:T(8,128)S(1)} %bitcast.2, f32[4,128,128]{2,1,0:T(8,128)S(1)} %copy-done.1, f32[3]{0:T(128)S(1)} %copy-done.2, f32[1]{0:T(128)S(6)} %copy.8.weight_ref), custom_call_target="tpu_custom_call" | custom-call | tf_op jit(solution)/shard_map/pallas_call | solution.py:563
  150.9 0.7 copy.9
  151.6 0.7 copy.10
Async XLA Ops:
  1.3 0.7 copy-start.2
  1.9 0.9 copy-start
  2.9 0.9 copy-start.1

commit v3 on v2

--- a/solution.py
+++ b/solution.py
@@ -204,11 +204,8 @@
         return mid, total
 
     def over(z0, count, step, body):
-        def one_step(i, _):
-            body(z0 + i * step)
-            return 0
-
-        lax.fori_loop(0, count // step, one_step, 0)
+        for z in range(z0, z0 + count, step):
+            body(z)
 
     def sweep(level, u, s, d, z, n, lo, rows):
         mid, total = neighbours(level, u, z, n, lo, rows)

time: 153 us -> 140 us (0.915)
  Pallas kernels: 147 us -> 135 us
    pallas_call x1, Pallas kernels: 147 us -> 135 us  [body(): pl.pallas_call(kernel, out_shape=(field, field), in_specs=[vmem, vmem, sm...]
where the time goes in v3:
time: 140 us
  Pallas kernels  135 us (96%)
  local copies, waits for them, and re-layouts  3.95 us (3%)
    pallas_call x1, Pallas kernels, body(): pl.pallas_call(kernel, out_shape=(field, field), in_specs=[vmem, vmem, sm...  135 us
    unnamed x8, local copies, waits for them, and re-layouts  3.95 us

profile of v3, /device:TPU:1, one launch (start us, length us, event | category | flops | bytes accessed | tf_op | source)
XLA Modules:
  0.0 139.9 jit_solution(15531723882176083485)
XLA Ops:
  1.3 0.0 copy-start.2
  1.3 0.6 copy-done.2
  1.9 0.0 copy-start
  1.9 0.9 copy-done
  2.9 0.0 copy-start.1
  2.9 0.9 copy-done.1
  3.8 134.7 %shard_map.59 = (f32[4,128,128]{2,1,0:T(8,128)S(1)}, f32[4,128,128]{2,1,0:T(8,128)S(1)}) custom-call(f32[4,128,128]{2,1,0:T(8,128)S(1)} %bitcast.2, f32[4,128,128]{2,1,0:T(8,128)S(1)} %copy-done.1, f32[3]{0:T(128)S(1)} %copy-done.2, f32[1]{0:T(128)S(6)} %copy.8.weight_ref), custom_call_target="tpu_custom_call" | custom-call | tf_op jit(solution)/shard_map/pallas_call | solution.py:560
  138.5 0.7 copy.9
  139.2 0.7 copy.10
Async XLA Ops:
  1.3 0.7 copy-start.2
  1.9 0.9 copy-start
  2.9 0.9 copy-start.1

commit v4 on v3

--- a/solution.py
+++ b/solution.py
@@ -10,15 +10,24 @@
 OMEGA = 0.8
 LANES = 128
 NZ, NY = 64, 128
-F32 = jnp.float32
+F32, BF16 = jnp.float32, jnp.bfloat16
 MESH = pl.DeviceIdType.MESH
+FARTHEST = sorted(range(1, 16), key=lambda d: -min(d // 4, 4 - d // 4) - min(d % 4, 4 - d % 4))
 DIRECTIONS = ((-1, 0), (1, 0), (0, -1), (0, 1), (-1, -1), (-1, 1), (1, -1), (1, 1))
 
 GEOMETRY = (dict(own_z=4, own_y=16, nz=16, ny=32), dict(own_z=5, own_y=12, nz=8, ny=16))
 
 
 def dot(a, b):
-    return jnp.dot(a, b, precision=lax.Precision.HIGHEST, preferred_element_type=F32)
+    high = a.astype(BF16)
+    rest = a - high.astype(F32)
+    middle = rest.astype(BF16)
+    low = (rest - middle.astype(F32)).astype(BF16)
+
+    def product(x):
+        return jnp.dot(x, b, preferred_element_type=F32)
+
+    return product(high) + (product(middle) + product(low))
 
 
 def flat(a):
@@ -32,7 +41,7 @@
 def kernel(
     vol_ref, reaction_ref, diff_ref, weight_ref, cent_out, mult_out,
     S0, SC, D0, DG0, UA, UB, U0a, U0b, C0, T0,
-    S1, S1C, D1, DG1, VA, VC, U1a, U1b, C1, T1, LZ, LY, LD,
+    S1, S1C, D1, DG1, VA, VC, U1a, U1b, C1, T1, P1, LZ, LY, LD, E0, LE, LQ,
     G, S2, D2, DG2, U2, T2, C2, D3,
     VB, MB, LB, XB, HB, PB, CB, WS, WB, IW,
     Rx, Rx1, R3, P3, E1, Px,
@@ -52,15 +61,48 @@
             src_ref=src, dst_ref=dst, send_sem=send, recv_sem=recv, device_id=to, device_id_type=MESH
         )
 
-    for ref in (SC, UA, UB, VA, VC, S1C, U0a, U0b, U1a, U1b, U2, LZ, LY, LD, T1):
+    for ref in (LZ, LY, LD, LE, LQ):
         ref[...] = jnp.zeros(ref.shape, F32)
     S0[...] = jnp.ones(S0.shape, F32)
 
     barrier = pltpu.get_barrier_semaphore()
-    for d in range(1, 16):
+    for d in FARTHEST:
         pl.semaphore_signal(barrier, inc=1, device_id=(member, at_slab(d // 4, d % 4)), device_id_type=MESH)
     for d in range(1, 8):
         pl.semaphore_signal(barrier, inc=1, device_id=(lax.rem(member + d, 8), slab), device_id_type=MESH)
+
+    coupling = [[diff_ref[i] * (0.25**level) for i in range(3)] for level in range(4)]
+    center = [2.0 * (c[0] + c[1] + c[2]) for c in coupling]
+
+    lane = lax.broadcasted_iota(jnp.int32, (1, LANES), 1)
+    one, zero = jnp.ones((1, LANES), F32), jnp.zeros((1, LANES), F32)
+
+    def lane_mask(keep):
+        return jnp.where(keep, one, zero)
+
+    row_i = lax.broadcasted_iota(jnp.int32, (LANES, LANES), 0)
+    col_i = lax.broadcasted_iota(jnp.int32, (LANES, LANES), 1)
+
+    def half(a):
+        return lax.shift_right_logical(a, 1)
+
+    def matrix(keep, value=1.0):
+        return jnp.where(keep, jnp.full((LANES, LANES), value, F32), jnp.zeros((LANES, LANES), F32)).astype(BF16)
+
+    Rx[...] = matrix(half(row_i) == col_i, 0.125)
+    Px[...] = matrix(row_i == half(col_i))
+    for q in range(4):
+        block = slice(LANES * q, LANES * q + LANES)
+        Rx1[block, :] = matrix((row_i < 64) & (half(row_i) + 32 * q == col_i), 0.125)
+        E1[:, block] = matrix((col_i < 64) & (row_i == half(col_i) + 32 * q))
+        R3[block, :] = matrix(16 * (2 * q + lax.shift_right_logical(row_i, 6)) + half(row_i & 31) == col_i, 0.125)
+        P3[:, block] = matrix(16 * (2 * q + lax.shift_right_logical(col_i, 6)) + half(col_i & 31) == row_i)
+
+    left = [lane_mask(lane > 0) * coupling[0][2], None, lane_mask((lane & 31) > 0) * coupling[2][2], lane_mask((lane & 15) > 0) * coupling[3][2]]
+    right = [lane_mask(lane < 127) * coupling[0][2], None, lane_mask((lane & 31) < 31) * coupling[2][2], lane_mask((lane & 15) < 15) * coupling[3][2]]
+    WS[...] = jnp.full((8, LANES), weight_ref[0], F32)
+    for ref in (SC, UA, UB, VA, VC, S1C, U0a, U0b, U1a, U1b, U2, T1):
+        ref[...] = jnp.zeros(ref.shape, F32)
     pl.semaphore_wait(barrier, 22)
 
     def inner(dz, dy):
@@ -69,16 +111,35 @@
     def halo0(slot):
         copies = []
         for k, (dz, dy) in enumerate(DIRECTIONS):
-            zs, zn, zd = {-1: (4, 3, 20), 0: (4, 16, 4), 1: (17, 3, 1)}[dz]
-            ys, yn, yd = {-1: (16, 8, 48), 0: (16, 32, 16), 1: (40, 8, 8)}[dy]
+            if dy == 0:
+                zs, zd = (4, 20) if dz < 0 else (17, 1)
+                src, dst = S0.at[slot, pl.ds(zs, 3), pl.ds(16, 32)], S0.at[slot, pl.ds(zd, 3), pl.ds(16, 32)]
+            elif dz == 0:
+                src, dst = E0.at[(dy + 1) // 2], LE.at[slot, k - 2]
+            else:
+                src, dst = E0.at[(dy + 1) // 2, pl.ds(0 if dz < 0 else 6, 2)], LQ.at[slot, k - 4]
             copies.append((
-                dz, dy,
-                remote(
-                    S0.at[slot, pl.ds(zs, zn), pl.ds(ys, yn)], S0.at[slot, pl.ds(zd, zn), pl.ds(yd, yn)],
-                    h0_send.at[slot, k], h0_recv.at[slot, k], (member, at_slab(dz, dy)),
-                ),
+                dz, dy, remote(src, dst, h0_send.at[slot, k], h0_recv.at[slot, k], (member, at_slab(dz, dy)))
             ))
         return copies
+
+    def begin_halo0(slot):
+        for edge, row in ((0, 16), (1, 44)):
+            for p in range(8):
+                E0[edge, p, 0:4, :] = S0[slot, 4 + 2 * p, row : row + 4, :]
+                E0[edge, p, 4:8, :] = S0[slot, 5 + 2 * p, row : row + 4, :]
+        begin_near(halo0(slot))
+
+    def finish_halo0(slot):
+        finish_near(halo0(slot))
+        for k, (dz, dy) in enumerate(DIRECTIONS):
+            if dy == 0:
+                continue
+            row, z0, tiles = (48 if dy < 0 else 12), {-1: 20, 0: 4, 1: 0}[dz], 8 if dz == 0 else 2
+            for p in range(tiles):
+                tile = LE[slot, k - 2, p] if dz == 0 else LQ[slot, k - 4, p]
+                S0[slot, z0 + 2 * p, row : row + 4, :] = tile[0:4]
+                S0[slot, z0 + 2 * p + 1, row : row + 4, :] = tile[4:8]
 
     def landing1(k, slot):
         if k < 2:
@@ -88,12 +149,12 @@
     def halo1(slot):
         copies = []
         for k, (dz, dy) in enumerate(DIRECTIONS):
-            z = {-1: pl.ds(4, 5), 0: pl.ds(4, 10), 1: pl.ds(9, 5)}[dz]
-            y = {-1: pl.ds(8, 8), 0: pl.ds(8, 24), 1: pl.ds(24, 8)}[dy]
+            z = {-1: pl.ds(0, 3), 0: pl.ds(0, 5), 1: pl.ds(2, 3)}[dz]
+            y = {-1: pl.ds(0, 8), 0: pl.ds(0, 24), 1: pl.ds(16, 8)}[dy]
             copies.append((
                 dz, dy,
                 remote(
-                    S1C.at[z, y], landing1(k, slot),
+                    P1.at[z, y], landing1(k, slot),
                     h1_send.at[slot, k], h1_recv.at[slot, k], (member, at_slab(dz, dy)),
                 ),
             ))
@@ -102,6 +163,11 @@
     def begin_near(copies):
         for dz, dy, c in copies:
             pl.when(inner(dz, dy))(c.start)
+
+    def begin_halo1(slot):
+        for p in range(5):
+            P1[p] = S1C[4 + 2 * p, 8:32, :] + lane_roll(S1C[5 + 2 * p, 8:32, :], 64)
+        begin_near(halo1(slot))
 
     def finish_near(copies):
         for dz, dy, c in copies:
@@ -115,7 +181,7 @@
                 G.at[slot, slab], G.at[slot, slab],
                 g_send.at[slot, d], g_recv.at[slot, d], (member, at_slab(d // 4, d % 4)),
             )
-            for d in range(1, 16)
+            for d in FARTHEST
         ]
 
     def begin(copies):
@@ -155,42 +221,9 @@
     reaction_moves = to_blocks(reaction_ref, S0.at[1], 4, 16, ra_send, ra_recv)
     volume_moves = to_blocks(vol_ref, VB, 0, 0, va_send, va_recv)
     begin(reaction_moves)
-    begin(volume_moves)
-    WS[...] = jnp.full((8, LANES), weight_ref[0], F32)
     weight_moves = [
         remote(WS, WB.at[d], w_send.at[d - 1], w_recv.at[d - 1], (lax.rem(member + d, 8), slab)) for d in range(1, 8)
     ]
-    begin(weight_moves)
-
-    coupling = [[diff_ref[i] * (0.25**level) for i in range(3)] for level in range(4)]
-    center = [2.0 * (c[0] + c[1] + c[2]) for c in coupling]
-
-    lane = lax.broadcasted_iota(jnp.int32, (1, LANES), 1)
-    one, zero = jnp.ones((1, LANES), F32), jnp.zeros((1, LANES), F32)
-
-    def lane_mask(keep):
-        return jnp.where(keep, one, zero)
-
-    row_i = lax.broadcasted_iota(jnp.int32, (LANES, LANES), 0)
-    col_i = lax.broadcasted_iota(jnp.int32, (LANES, LANES), 1)
-
-    def half(a):
-        return lax.shift_right_logical(a, 1)
-
-    def matrix(keep, value=1.0):
-        return jnp.where(keep, jnp.full((LANES, LANES), value, F32), jnp.zeros((LANES, LANES), F32))
-
-    Rx[...] = matrix(half(row_i) == col_i, 0.125)
-    Px[...] = matrix(row_i == half(col_i))
-    for q in range(4):
-        block = slice(LANES * q, LANES * q + LANES)
-        Rx1[block, :] = matrix((row_i < 64) & (half(row_i) + 32 * q == col_i), 0.125)
-        E1[:, block] = matrix((col_i < 64) & (row_i == half(col_i) + 32 * q))
-        R3[block, :] = matrix(16 * (2 * q + lax.shift_right_logical(row_i, 6)) + half(row_i & 31) == col_i, 0.125)
-        P3[:, block] = matrix(16 * (2 * q + lax.shift_right_logical(col_i, 6)) + half(col_i & 31) == row_i)
-
-    left = [lane_mask(lane > 0) * coupling[0][2], None, lane_mask((lane & 31) > 0) * coupling[2][2], lane_mask((lane & 15) > 0) * coupling[3][2]]
-    right = [lane_mask(lane < 127) * coupling[0][2], None, lane_mask((lane & 31) < 31) * coupling[2][2], lane_mask((lane & 15) < 15) * coupling[3][2]]
 
     def neighbours(level, u, z, n, lo, rows):
         c = coupling[level]
@@ -240,18 +273,23 @@
         own = jnp.concatenate([e[2], e[3], e[4], e[5]], axis=1)
         sides = jnp.concatenate([e[6], e[7], e[0], e[1]], axis=1)
         m = dot(jnp.concatenate([own, sides], axis=0), Rx1[...]).reshape(2, 16, LANES)
-        G[slot, slab, :, 0:8, :] = m[:, 4:12]
-        G[slot, slab, :, 8:12, :] = m[:, 12:16]
-        G[slot, slab, :, 12:16, :] = m[:, 0:4]
-
-    upper_half, upper_rows = lane >= 64, lax.broadcasted_iota(jnp.int32, (8, LANES), 0) < 4
+        G[slot, slab, 0:8, :] = m[0, 4:12]
+        G[slot, slab, 8:16, :] = m[1, 4:12]
+        for row, part in ((16, m[0, 12:14]), (18, m[1, 12:14]), (20, m[1, 2:4]), (22, m[0, 2:4])):
+            G[slot, slab, row : row + 2, :] = part
+
+    upper_half, row8 = lane >= 64, lax.broadcasted_iota(jnp.int32, (8, LANES), 0)
     nothing = jnp.zeros((8, LANES), F32)
 
     def gathered(slot):
         def rows(c, j, g):
-            below = G[slot, 4 * c + j - 1, g, 8:16, :] if j > 0 else nothing
-            above = G[slot, 4 * c + j + 1, g, 8:16, :] if j < 3 else nothing
-            return G[slot, 4 * c + j, g, 0:8, :] + jnp.where(upper_rows, below, above)
+            below = G[slot, 4 * c + j - 1, 16:24, :] if j > 0 else nothing
+            above = G[slot, 4 * c + j + 1, 16:24, :] if j < 3 else nothing
+            if g:
+                below = pltpu.roll(below, 6, 0) if j > 0 else nothing
+                above = pltpu.roll(above, 2, 0) if j < 3 else nothing
+            near = jnp.where(row8 < 2, below, jnp.where(row8 >= 6, above, nothing))
+            return G[slot, 4 * c + j, 8 * g : 8 * g + 8, :] + near
 
         for j in range(4):
             side = [nothing] + [rows(c, j, 1) for c in range(4)] + [nothing]
@@ -309,23 +347,29 @@
     finish(reaction_moves)
     mine = pl.ds(pl.multiple_of(32 * cy, 32), 32)
     S0[1, pl.ds(4 + 4 * cy, 4), 16:48, :] = reaction_ref[:, mine, :]
-    begin_near(halo0(1))
+    begin_halo0(1)
     SC[4:20, 16:48, :] = S0[1, 4:20, 16:48, :]
     restrict0(lambda z: SC[pl.ds(z, 4), 8:56, :])
     restrict1(lambda z: S1C[pl.ds(z, 8), 8:32, :], 1)
     begin(gather(1))
-    begin_near(halo1(1))
+    begin_halo1(1)
+    begin(volume_moves)
+    begin(weight_moves)
     VB[pl.ds(4 * cy, 4)] = vol_ref[:, mine, :]
 
     def summed1(slot):
         finish_near(halo1(slot))
         S1[1:17, 8:32, :] = S1C[1:17, 8:32, :]
         for k, (dz, dy) in enumerate(DIRECTIONS):
-            z = {-1: slice(12, 17), 0: slice(4, 14), 1: slice(1, 6)}[dz]
+            z0, tiles = {-1: (12, 3), 0: (4, 5), 1: (0, 3)}[dz]
             y = {-1: slice(24, 32), 0: slice(8, 32), 1: slice(8, 16)}[dy]
-            S1[z, y, :] += landing1(k, slot)[...]
-
-    finish_near(halo0(1))
+            for p in range(tiles):
+                both = landing1(k, slot)[p]
+                for z, part in ((z0 + 2 * p, both), (z0 + 2 * p + 1, lane_roll(both, 64))):
+                    if 1 <= z < 17:
+                        S1[z, y, :] += jnp.where(upper_half, jnp.zeros_like(part), part)
+
+    finish_halo0(1)
 
     def diag0(z):
         diag = S0[1, pl.ds(z, 2), 8:56, :] + center[0]
@@ -362,6 +406,7 @@
 
         over(3, 18, 3, own0)
         restrict0(lambda z: residual(0, UB, SC, DG0, z, 4, 8, 48))
+        begin_halo1(slot)
         VA[4:14, 8:32, :] = D1[4:14, 8:32, :] * S1C[4:14, 8:32, :]
 
         def own1(z):
@@ -370,11 +415,10 @@
         over(3, 12, 6, own1)
         restrict1(lambda z: residual(1, VC, S1C, DG1, z, 8, 8, 24), slot)
         begin(gather(slot))
-        begin_near(halo1(slot))
 
         @pl.when(n > 0)
         def _():
-            finish_near(halo0(slot))
+            finish_halo0(slot)
 
         source0 = S0.at[slot]
 
@@ -451,10 +495,27 @@
 
         over(4, 16, 4, post0b)
 
-    def centroid():
+    def centroid(last):
         sibling = (member + 1 - 2 * mc, slab)
         swap = remote(LB.at[pl.ds(8 * (1 - mc), 8)], XB, x_send, x_recv, sibling)
+
+        def marginal(at):
+            m = S0[0, pl.ds(4 + at, 4), 16:48, :] * MB[pl.ds(at, 4)]
+            MB[pl.ds(at, 4)] = m
+            LB[pl.ds(at, 4)] = weight_ref[0] * jnp.log(m)
+
+        def update(at, planes):
+            for k in range(0, planes, 2):
+                z = pl.ds(at + k, 2)
+                p = S0[0, pl.ds(4 + at + k, 2), 16:48, :] * CB[z] / MB[z]
+                S0[0, pl.ds(4 + at + k, 2), 16:48, :] = p
+                SC[pl.ds(4 + at + k, 2), 16:48, :] = p
+
+        marginal(8 * (1 - mc))
+        marginal(8 * (1 - mc) + 4)
         swap.start()
+        marginal(8 * mc)
+        marginal(8 * mc + 4)
         swap.wait()
         HB[...] = LB[pl.ds(8 * mc, 8)] + XB[...]
         pieces = []
@@ -480,12 +541,30 @@
             passed.append(remote(CB.at[pl.ds(at, 2)], CB.at[pl.ds(at, 2)], f_send.at[d], f_recv.at[d], sibling))
         begin(spread)
         passed[0].start()
+        update(own, 2)
         for d in range(1, 4):
             spread[d - 1].wait_recv()
             passed[d].start()
-        for c in spread:
+            update(8 * mc + 2 * lax.rem(mx - d + 4, 4), 2)
+        for d in range(4):
+            passed[d].wait_recv()
+        pl.when(last)(lambda: begin(centroid_moves()))
+        update(8 * (1 - mc), 8)
+        for c in spread + passed:
             c.wait_send()
-        finish(passed)
+
+    def centroid_moves():
+        copies = []
+        for d in range(1, 4):
+            to = lax.rem(cy + d, 4)
+            copies.append(
+                remote(
+                    CB.at[pl.ds(4 * to + 2 * mc, 2)],
+                    cent_out.at[pl.ds(2 * mc, 2), pl.ds(pl.multiple_of(32 * cy, 32), 32)],
+                    o_send.at[0, d - 1], o_recv.at[0, d - 1], (member, cz * 4 + to),
+                )
+            )
+        return copies
 
     def half_step(n, _):
         slot = lax.rem(n, 2)
@@ -506,36 +585,26 @@
 
         @pl.when(slot == 1)
         def _():
-            def marginal(z):
-                m = S0[0, pl.ds(z, 4), 16:48, :] * MB[pl.ds(z - 4, 4)]
-                MB[pl.ds(z - 4, 4)] = m
-                LB[pl.ds(z - 4, 4)] = weight_ref[0] * jnp.log(m)
-
-            over(4, 16, 4, marginal)
-            centroid()
-
-            def update(z):
-                p = S0[0, pl.ds(z, 4), 16:48, :] * CB[pl.ds(z - 4, 4)] / MB[pl.ds(z - 4, 4)]
-                S0[0, pl.ds(z, 4), 16:48, :] = p
-                SC[pl.ds(z, 4), 16:48, :] = p
-
-            over(4, 16, 4, update)
+            centroid(n == 2 * ITERS - 1)
 
         @pl.when(n < 2 * ITERS - 1)
         def _():
-            begin_near(halo0(1 - slot))
+            begin_halo0(1 - slot)
 
         return 0
 
     lax.fori_loop(0, 2 * ITERS, half_step, 0)
 
-    moves = to_slabs(CB, 0, 0, cent_out, o_send.at[0], o_recv.at[0]) + to_slabs(
-        S0.at[0], 4, 16, mult_out, o_send.at[1], o_recv.at[1]
-    )
+    moves = to_slabs(S0.at[0], 4, 16, mult_out, o_send.at[1], o_recv.at[1])
     begin(moves)
-    cent_out[:, mine, :] = CB[pl.ds(4 * cy, 4)]
     mult_out[:, mine, :] = S0[0, pl.ds(4 + 4 * cy, 4), 16:48, :]
+    cent_out[pl.ds(2 * mc, 2), mine, :] = CB[pl.ds(4 * cy + 2 * mc, 2)]
+    finish(centroid_moves())
+    half_out = cent_out.at[pl.ds(2 * mc, 2)]
+    across = remote(half_out, half_out, x_send, x_recv, (member + 1 - 2 * mc, slab))
+    across.start()
     finish(moves)
+    across.wait()
 
 
 def body(nonnegative_volumes, reaction, diffusivity, member_weights):
@@ -548,11 +617,12 @@
     dma = pltpu.SemaphoreType.DMA
     scratch = [
         buffer(2, 24, 64), *[buffer(24, 64) for _ in range(7)], buffer(5, 48), buffer(10, 48),
-        *[buffer(18, 40) for _ in range(8)], buffer(8, 32), buffer(8, 32), buffer(2, 2, 5, 24), buffer(2, 2, 10, 8), buffer(2, 4, 5, 8),
-        buffer(2, 16, 2, 16), buffer(4, 32), buffer(4, 32), buffer(4, 32), buffer(6, 48), buffer(4, 32), buffer(4, 32), buffer(16),
+        *[buffer(18, 40) for _ in range(8)], buffer(8, 32), buffer(8, 32), buffer(5, 24),
+        buffer(2, 2, 3, 24), buffer(2, 2, 5, 8), buffer(2, 4, 3, 8), buffer(2, 8, 8), buffer(2, 2, 8, 8), buffer(2, 4, 2, 8),
+        buffer(2, 16, 24), buffer(4, 32), buffer(4, 32), buffer(4, 32), buffer(6, 48), buffer(4, 32), buffer(4, 32), buffer(16),
         buffer(16, 32), buffer(16, 32), buffer(16, 32), buffer(8, 32), buffer(8, 32), buffer(3, 2, 32), buffer(16, 32),
         buffer(8), buffer(8, 8), buffer(8),
-        buffer(128), buffer(512), buffer(512), pltpu.VMEM((128, 512), F32), pltpu.VMEM((128, 512), F32), buffer(128),
+        *[pltpu.VMEM(shape, BF16) for shape in ((128, 128), (512, 128), (512, 128), (128, 512), (128, 512), (128, 128))],
         dma((2, 8)), dma((2, 8)), dma((2, 8)), dma((2, 8)), dma((2, 16)), dma((2, 16)),
         dma((3,)), dma((3,)), dma((3,)), dma((3,)), dma((7,)), dma((7,)),
         dma, dma, dma((3,)), dma((3,)), dma((3,)), dma((3,)), dma((4,)), dma((4,)), dma((2, 3)), dma((2, 3)),

time: 140 us -> 125 us (0.89)
  Pallas kernels: 135 us -> 119 us
    pallas_call x1, Pallas kernels: 135 us -> 119 us  [body(): pl.pallas_call(kernel, out_shape=(field, field), in_specs=[vmem, vmem, sm...]
where the time goes in v4:
time: 125 us; the launch traced here: 124 us
  Pallas kernels  119 us (95%)
  local copies, waits for them, and re-layouts  3.95 us (3%)
  between operations  1.3 us (1%)
    pallas_call x1, Pallas kernels, body(): pl.pallas_call(kernel, out_shape=(field, field), in_specs=[vmem, vmem, sm...  119 us
    unnamed x8, local copies, waits for them, and re-layouts  3.95 us

profile of v4, /device:TPU:1, one launch (start us, length us, event | category | flops | bytes accessed | tf_op | source)
XLA Modules:
  0.0 124.5 jit_solution(8321693994077095645)
XLA Ops:
  1.3 0.0 copy-start.2
  1.3 0.6 copy-done.2
  1.9 0.0 copy-start
  1.9 0.9 copy-done
  2.9 0.0 copy-start.1
  2.9 0.9 copy-done.1
  3.8 119.2 %shard_map.59 = (f32[4,128,128]{2,1,0:T(8,128)S(1)}, f32[4,128,128]{2,1,0:T(8,128)S(1)}) custom-call(f32[4,128,128]{2,1,0:T(8,128)S(1)} %bitcast.2, f32[4,128,128]{2,1,0:T(8,128)S(1)} %copy-done.1, f32[3]{0:T(128)S(1)} %copy-done.2, f32[1]{0:T(128)S(6)} %copy.8.weight_ref), custom_call_target="tpu_custom_call" | custom-call | tf_op jit(solution)/shard_map/pallas_call | solution.py:630
  123.1 0.7 copy.9
  123.8 0.7 copy.10
Async XLA Ops:
  1.3 0.7 copy-start.2
  1.9 0.9 copy-start
  2.9 0.9 copy-start.1

commit v5 on v4

--- a/solution.py
+++ b/solution.py
@@ -20,14 +20,8 @@
 
 def dot(a, b):
     high = a.astype(BF16)
-    rest = a - high.astype(F32)
-    middle = rest.astype(BF16)
-    low = (rest - middle.astype(F32)).astype(BF16)
-
-    def product(x):
-        return jnp.dot(x, b, preferred_element_type=F32)
-
-    return product(high) + (product(middle) + product(low))
+    low = (a - high.astype(F32)).astype(BF16)
+    return jnp.dot(high, b, preferred_element_type=F32) + jnp.dot(low, b, preferred_element_type=F32)
 
 
 def flat(a):
@@ -42,12 +36,12 @@
     vol_ref, reaction_ref, diff_ref, weight_ref, cent_out, mult_out,
     S0, SC, D0, DG0, UA, UB, U0a, U0b, C0, T0,
     S1, S1C, D1, DG1, VA, VC, U1a, U1b, C1, T1, P1, LZ, LY, LD, E0, LE, LQ,
-    G, S2, D2, DG2, U2, T2, C2, D3,
+    G, S2, D2, DG2, U2, T2, C2, D3, K3,
     VB, MB, LB, XB, HB, PB, CB, WS, WB, IW,
     Rx, Rx1, R3, P3, E1, Px,
     h0_send, h0_recv, h1_send, h1_recv, g_send, g_recv,
     ra_send, ra_recv, va_send, va_recv, w_send, w_recv,
-    x_send, x_recv, p_send, p_recv, c_send, c_recv, f_send, f_recv, o_send, o_recv,
+    l_sem, x_send, x_recv, p_send, p_recv, c_send, c_recv, f_send, f_recv, o_send, o_recv,
 ):
     member, slab = lax.axis_index("member"), lax.axis_index("slab")
     cz, cy = slab // 4, lax.rem(slab, 4)
@@ -64,6 +58,11 @@
     for ref in (LZ, LY, LD, LE, LQ):
         ref[...] = jnp.zeros(ref.shape, F32)
     S0[...] = jnp.ones(S0.shape, F32)
+    mine = pl.ds(pl.multiple_of(32 * cy, 32), 32)
+    own_reaction = pltpu.make_async_copy(reaction_ref.at[:, mine], S0.at[1, pl.ds(4 + 4 * cy, 4), pl.ds(16, 32)], l_sem.at[0])
+    own_volume = pltpu.make_async_copy(vol_ref.at[:, mine], VB.at[pl.ds(4 * cy, 4)], l_sem.at[1])
+    own_reaction.start()
+    own_volume.start()
 
     barrier = pltpu.get_barrier_semaphore()
     for d in FARTHEST:
@@ -325,14 +324,20 @@
     before3 = lane_mask(lane >= 16) * coupling[3][0]
     after3 = lane_mask(lane < 112) * coupling[3][0]
 
+    def coefficients3(d):
+        for i, c in enumerate((before3, after3, up3, down3, left[3], right[3])):
+            K3[i] = d * c
+        D3[...] = d
+
     def level3(s):
-        d = D3[...]
-        u = d * s
+        k = [K3[i] for i in range(6)]
+        base = D3[...] * s
+        u = base
         for _ in range(COARSE_SWEEPS - 1):
-            total = before3 * lane_roll(u, 16) + after3 * lane_roll(u, -16)
-            total += up3 * pltpu.roll(u, 1, 0) + down3 * pltpu.roll(u, 15, 0)
-            total += left[3] * lane_roll(u, 1) + right[3] * lane_roll(u, -1)
-            u = (1.0 - OMEGA) * u + d * (s + total)
+            z = k[0] * lane_roll(u, 16) + k[1] * lane_roll(u, -16)
+            y = k[2] * pltpu.roll(u, 1, 0) + k[3] * pltpu.roll(u, 15, 0)
+            x = k[4] * lane_roll(u, 1) + k[5] * lane_roll(u, -1)
+            u = (base + (1.0 - OMEGA) * u + y) + (z + x)
         return u
 
     def inside(level, z, n, lo, rows):
@@ -345,8 +350,7 @@
         return keep
 
     finish(reaction_moves)
-    mine = pl.ds(pl.multiple_of(32 * cy, 32), 32)
-    S0[1, pl.ds(4 + 4 * cy, 4), 16:48, :] = reaction_ref[:, mine, :]
+    own_reaction.wait()
     begin_halo0(1)
     SC[4:20, 16:48, :] = S0[1, 4:20, 16:48, :]
     restrict0(lambda z: SC[pl.ds(z, 4), 8:56, :])
@@ -355,7 +359,7 @@
     begin_halo1(1)
     begin(volume_moves)
     begin(weight_moves)
-    VB[pl.ds(4 * cy, 4)] = vol_ref[:, mine, :]
+    own_volume.wait()
 
     def summed1(slot):
         finish_near(halo1(slot))
@@ -389,7 +393,7 @@
     gathered(1)
     DG2[...] = S2[...] + center[2]
     D2[...] = OMEGA / DG2[...]
-    D3[...] = OMEGA / (restrict2(S2[...]) + center[3])
+    coefficients3(OMEGA / (restrict2(S2[...]) + center[3]))
     SC[4:20, 16:48, :] = jnp.ones((16, 32, LANES), F32)
     finish(volume_moves)
     finish(weight_moves)
@@ -497,61 +501,74 @@
 
     def centroid(last):
         sibling = (member + 1 - 2 * mc, slab)
-        swap = remote(LB.at[pl.ds(8 * (1 - mc), 8)], XB, x_send, x_recv, sibling)
 
         def marginal(at):
             m = S0[0, pl.ds(4 + at, 4), 16:48, :] * MB[pl.ds(at, 4)]
             MB[pl.ds(at, 4)] = m
             LB[pl.ds(at, 4)] = weight_ref[0] * jnp.log(m)
 
-        def update(at, planes):
-            for k in range(0, planes, 2):
-                z = pl.ds(at + k, 2)
-                p = S0[0, pl.ds(4 + at + k, 2), 16:48, :] * CB[z] / MB[z]
-                S0[0, pl.ds(4 + at + k, 2), 16:48, :] = p
-                SC[pl.ds(4 + at + k, 2), 16:48, :] = p
-
-        marginal(8 * (1 - mc))
-        marginal(8 * (1 - mc) + 4)
-        swap.start()
-        marginal(8 * mc)
-        marginal(8 * mc + 4)
-        swap.wait()
-        HB[...] = LB[pl.ds(8 * mc, 8)] + XB[...]
-        pieces = []
+        def update(at):
+            p = S0[0, 4 + at, 16:48, :] * CB[at] / MB[at]
+            S0[0, 4 + at, 16:48, :] = p
+            SC[4 + at, 16:48, :] = p
+
+        def along_x(d):
+            return (2 * lax.rem(mx + d, 4) + mc, slab)
+
+        swaps, pieces, spread, passed = [], [], [], []
+        for q in range(2):
+            marginal(8 * q + 4 * (1 - mc))
+            theirs, here = LB.at[pl.ds(8 * q + 4 * (1 - mc), 4)], XB.at[pl.ds(4 * q, 4)]
+            swaps.append(remote(theirs, here, x_send.at[q], x_recv.at[q], sibling))
+            swaps[q].start()
+        for q in range(2):
+            marginal(8 * q + 4 * mc)
+        for q in range(2):
+            swaps[q].wait_recv()
+            HB[4 * q : 4 * q + 4] = LB[pl.ds(8 * q + 4 * mc, 4)] + XB[4 * q : 4 * q + 4]
+            pieces.append([])
+            for d in (2, 1, 3):
+                part = HB.at[pl.ds(4 * q + lax.rem(mx + d, 4), 1)]
+                pieces[q].append(remote(part, PB.at[q, d - 1], p_send.at[q, d - 1], p_recv.at[q, d - 1], along_x(d)))
+            begin(pieces[q])
+        inverse = jnp.broadcast_to(IW[...][None], (4, 8, LANES)).reshape(1, 32, LANES)
+        for q in range(2):
+            for c in pieces[q]:
+                c.wait_recv()
+            total = HB[pl.ds(4 * q + mx, 1)] + PB[q, 0] + PB[q, 1] + PB[q, 2]
+            own = 8 * q + 4 * mc + mx
+            CB[pl.ds(own, 1)] = jnp.exp(total * inverse)
+            made = CB.at[pl.ds(own, 1)]
+            spread.append([remote(made, made, c_send.at[q, d - 1], c_recv.at[q, d - 1], along_x(d)) for d in (2, 1, 3)])
+            begin(spread[q])
+            passed.append([])
+            for d in (0, 1, 3, 2):
+                at = CB.at[pl.ds(8 * q + 4 * mc + lax.rem(mx - d + 4, 4), 1)]
+                passed[q].append((d, remote(at, at, f_send.at[q, d], f_recv.at[q, d], sibling)))
+            passed[q][0][1].start()
+            update(own)
+        for q in range(2):
+            for (d, c), arrived in zip(passed[q][1:], spread[q][1:] + spread[q][:1]):
+                arrived.wait_recv()
+                c.start()
+                update(8 * q + 4 * mc + lax.rem(mx - d + 4, 4))
         for d in range(1, 4):
-            to = lax.rem(mx + d, 4)
-            pieces.append(
-                remote(HB.at[pl.ds(2 * to, 2)], PB.at[d - 1], p_send.at[d - 1], p_recv.at[d - 1], (2 * to + mc, slab))
-            )
-        begin(pieces)
-        finish(pieces)
-        total = HB[pl.ds(2 * mx, 2)] + PB[0] + PB[1] + PB[2]
-        inverse = jnp.broadcast_to(IW[...][None, None], (2, 4, 8, LANES)).reshape(2, 32, LANES)
-        own = 8 * mc + 2 * mx
-        CB[pl.ds(own, 2)] = jnp.exp(total * inverse)
-        spread, passed = [], []
+            to = lax.rem(cy + d, 4)
+            pl.when(last & (lax.rem(to, 2) == mc))(multiplier_moves()[d - 1].start)
+        for q in range(2):
+            for d, c in passed[q]:
+                c.wait_recv()
+                update(8 * q + 4 * (1 - mc) + lax.rem(mx - d + 4, 4))
         for d in range(1, 4):
-            to = lax.rem(mx + d, 4)
-            spread.append(
-                remote(CB.at[pl.ds(own, 2)], CB.at[pl.ds(own, 2)], c_send.at[d - 1], c_recv.at[d - 1], (2 * to + mc, slab))
-            )
-        for d in range(4):
-            at = 8 * mc + 2 * lax.rem(mx - d + 4, 4)
-            passed.append(remote(CB.at[pl.ds(at, 2)], CB.at[pl.ds(at, 2)], f_send.at[d], f_recv.at[d], sibling))
-        begin(spread)
-        passed[0].start()
-        update(own, 2)
-        for d in range(1, 4):
-            spread[d - 1].wait_recv()
-            passed[d].start()
-            update(8 * mc + 2 * lax.rem(mx - d + 4, 4), 2)
-        for d in range(4):
-            passed[d].wait_recv()
+            to = lax.rem(cy + d, 4)
+            pl.when(last & (lax.rem(to, 2) != mc))(multiplier_moves()[d - 1].start)
         pl.when(last)(lambda: begin(centroid_moves()))
-        update(8 * (1 - mc), 8)
-        for c in spread + passed:
-            c.wait_send()
+        for q in range(2):
+            for c in [swaps[q]] + pieces[q] + spread[q] + [f for _, f in passed[q]]:
+                c.wait_send()
+
+    def multiplier_moves():
+        return to_slabs(S0.at[0], 4, 16, mult_out, o_send.at[1], o_recv.at[1])
 
     def centroid_moves():
         copies = []
@@ -595,20 +612,19 @@
 
     lax.fori_loop(0, 2 * ITERS, half_step, 0)
 
-    moves = to_slabs(S0.at[0], 4, 16, mult_out, o_send.at[1], o_recv.at[1])
-    begin(moves)
     mult_out[:, mine, :] = S0[0, pl.ds(4 + 4 * cy, 4), 16:48, :]
     cent_out[pl.ds(2 * mc, 2), mine, :] = CB[pl.ds(4 * cy + 2 * mc, 2)]
     finish(centroid_moves())
     half_out = cent_out.at[pl.ds(2 * mc, 2)]
-    across = remote(half_out, half_out, x_send, x_recv, (member + 1 - 2 * mc, slab))
+    across = remote(half_out, half_out, x_send.at[0], x_recv.at[0], (member + 1 - 2 * mc, slab))
     across.start()
-    finish(moves)
+    finish(multiplier_moves())
     across.wait()
 
 
 def body(nonnegative_volumes, reaction, diffusivity, member_weights):
     vmem, smem = pl.BlockSpec(memory_space=pltpu.VMEM), pl.BlockSpec(memory_space=pltpu.SMEM)
+    hbm = pl.BlockSpec(memory_space=pl.ANY)
     field = jax.ShapeDtypeStruct((4, 128, 128), F32)
 
     def buffer(*shape):
@@ -619,18 +635,18 @@
         buffer(2, 24, 64), *[buffer(24, 64) for _ in range(7)], buffer(5, 48), buffer(10, 48),
         *[buffer(18, 40) for _ in range(8)], buffer(8, 32), buffer(8, 32), buffer(5, 24),
         buffer(2, 2, 3, 24), buffer(2, 2, 5, 8), buffer(2, 4, 3, 8), buffer(2, 8, 8), buffer(2, 2, 8, 8), buffer(2, 4, 2, 8),
-        buffer(2, 16, 24), buffer(4, 32), buffer(4, 32), buffer(4, 32), buffer(6, 48), buffer(4, 32), buffer(4, 32), buffer(16),
-        buffer(16, 32), buffer(16, 32), buffer(16, 32), buffer(8, 32), buffer(8, 32), buffer(3, 2, 32), buffer(16, 32),
+        buffer(2, 16, 24), buffer(4, 32), buffer(4, 32), buffer(4, 32), buffer(6, 48), buffer(4, 32), buffer(4, 32), buffer(16), buffer(6, 16),
+        buffer(16, 32), buffer(16, 32), buffer(16, 32), buffer(8, 32), buffer(8, 32), buffer(2, 3, 1, 32), buffer(16, 32),
         buffer(8), buffer(8, 8), buffer(8),
         *[pltpu.VMEM(shape, BF16) for shape in ((128, 128), (512, 128), (512, 128), (128, 512), (128, 512), (128, 128))],
         dma((2, 8)), dma((2, 8)), dma((2, 8)), dma((2, 8)), dma((2, 16)), dma((2, 16)),
         dma((3,)), dma((3,)), dma((3,)), dma((3,)), dma((7,)), dma((7,)),
-        dma, dma, dma((3,)), dma((3,)), dma((3,)), dma((3,)), dma((4,)), dma((4,)), dma((2, 3)), dma((2, 3)),
+        dma((2,)), dma((2,)), dma((2,)), *[dma((2, 3)) for _ in range(4)], dma((2, 4)), dma((2, 4)), dma((2, 3)), dma((2, 3)),
     ]
     centroid, multipliers = pl.pallas_call(
         kernel,
         out_shape=(field, field),
-        in_specs=[vmem, vmem, smem, smem],
+        in_specs=[hbm, hbm, smem, smem],
         out_specs=(vmem, vmem),
         scratch_shapes=scratch,
         compiler_params=pltpu.CompilerParams(collective_id=0, has_side_effects=True, vmem_limit_bytes=40 * 2**20),

time: 125 us -> 121 us (0.968)
  Pallas kernels: 119 us -> 116 us
    pallas_call x1, Pallas kernels: 119 us -> 116 us  [body(): pl.pallas_call(kernel, out_shape=(field, field), in_specs=[hbm, hbm, smem...]
where the time goes in v5:
time: 121 us
  Pallas kernels  116 us (96%)
  local copies, waits for them, and re-layouts  3.95 us (3%)
  between operations  1.3 us (1%)
    pallas_call x1, Pallas kernels, body(): pl.pallas_call(kernel, out_shape=(field, field), in_specs=[hbm, hbm, smem...  116 us
    unnamed x8, local copies, waits for them, and re-layouts  3.95 us

profile of v5, /device:TPU:1, one launch (start us, length us, event | category | flops | bytes accessed | tf_op | source)
XLA Modules:
  0.0 120.9 jit_solution(15320740416077403157)
XLA Ops:
  1.3 0.0 copy-start.2
  1.3 0.6 copy-done.2
  1.9 0.0 copy-start
  1.9 0.9 copy-done
  2.9 0.0 copy-start.1
  2.9 0.9 copy-done.1
  3.8 115.7 %shard_map.59 = (f32[4,128,128]{2,1,0:T(8,128)S(1)}, f32[4,128,128]{2,1,0:T(8,128)S(1)}) custom-call(f32[4,128,128]{2,1,0:T(8,128)S(1)} %bitcast.2, f32[4,128,128]{2,1,0:T(8,128)S(1)} %copy-done.1, f32[3]{0:T(128)S(1)} %copy-done.2, f32[1]{0:T(128)S(6)} %copy.8.weight_ref), custom_call_target="tpu_custom_call" | custom-call | tf_op jit(solution)/shard_map/pallas_call | solution.py:646
  119.5 0.7 copy.9
  120.2 0.7 copy.10
Async XLA Ops:
  1.3 0.7 copy-start.2
  1.9 0.9 copy-start
  2.9 0.9 copy-start.1

commit v6 on v5

--- a/solution.py
+++ b/solution.py
@@ -41,7 +41,7 @@
     Rx, Rx1, R3, P3, E1, Px,
     h0_send, h0_recv, h1_send, h1_recv, g_send, g_recv,
     ra_send, ra_recv, va_send, va_recv, w_send, w_recv,
-    l_sem, x_send, x_recv, p_send, p_recv, c_send, c_recv, f_send, f_recv, o_send, o_recv,
+    l_sem, x_send, x_recv, p_send, p_recv, c_send, c_recv, f_send, f_recv, o_send, o_recv, e_send, e_recv, k_send, k_recv,
 ):
     member, slab = lax.axis_index("member"), lax.axis_index("slab")
     cz, cy = slab // 4, lax.rem(slab, 4)
@@ -116,7 +116,7 @@
             elif dz == 0:
                 src, dst = E0.at[(dy + 1) // 2], LE.at[slot, k - 2]
             else:
-                src, dst = E0.at[(dy + 1) // 2, pl.ds(0 if dz < 0 else 6, 2)], LQ.at[slot, k - 4]
+                src, dst = E0.at[(dy + 1) // 2, pl.ds(0 if dz < 0 else 7, 1)], LQ.at[slot, k - 4]
             copies.append((
                 dz, dy, remote(src, dst, h0_send.at[slot, k], h0_recv.at[slot, k], (member, at_slab(dz, dy)))
             ))
@@ -134,7 +134,7 @@
         for k, (dz, dy) in enumerate(DIRECTIONS):
             if dy == 0:
                 continue
-            row, z0, tiles = (48 if dy < 0 else 12), {-1: 20, 0: 4, 1: 0}[dz], 8 if dz == 0 else 2
+            row, z0, tiles = (48 if dy < 0 else 12), {-1: 20, 0: 4, 1: 2}[dz], 8 if dz == 0 else 1
             for p in range(tiles):
                 tile = LE[slot, k - 2, p] if dz == 0 else LQ[slot, k - 4, p]
                 S0[slot, z0 + 2 * p, row : row + 4, :] = tile[0:4]
@@ -178,10 +178,18 @@
         return [
             remote(
                 G.at[slot, slab], G.at[slot, slab],
-                g_send.at[slot, d], g_recv.at[slot, d], (member, at_slab(d // 4, d % 4)),
+                g_send.at[slot], g_recv.at[slot], (member, at_slab(d // 4, d % 4)),
             )
             for d in FARTHEST
         ]
+
+    def finish_gather(slot):
+        all_of_them = G.at[slot, 0:15]
+        pltpu.make_async_copy(all_of_them, all_of_them, g_recv.at[slot]).wait()
+
+    def finish_gather_sends(slot):
+        all_of_them = G.at[slot, 0:15]
+        pltpu.make_async_copy(all_of_them, all_of_them, g_send.at[slot]).wait()
 
     def begin(copies):
         for c in copies:
@@ -389,7 +397,8 @@
         D1[pl.ds(z, 2), 8:32, :] = jnp.where(inside(1, z, 2, 8, 24), OMEGA / diag, jnp.zeros((2, 24, LANES), F32))
 
     over(1, 16, 2, diag1)
-    finish(gather(1))
+    finish_gather(1)
+    finish_gather_sends(1)
     gathered(1)
     DG2[...] = S2[...] + center[2]
     D2[...] = OMEGA / DG2[...]
@@ -443,7 +452,7 @@
 
         over(2, 14, 7, pre1)
 
-        finish(gather(slot))
+        finish_gather(slot)
         gathered(slot)
         U2[1:5, 8:40, :] = D2[...] * S2[...]
         sweep2()
@@ -457,6 +466,8 @@
         sweep2()
         sweep2()
 
+        finish_gather_sends(slot)
+
         window = pl.ds(pl.multiple_of(8 * cy, 8), 24)
         own = U2[1 + cz, window, :][4:20]
         sides = jnp.where(upper_half, U2[cz, window, :][4:20], U2[2 + cz, window, :][4:20])
@@ -523,6 +534,12 @@
             swaps[q].start()
         for q in range(2):
             marginal(8 * q + 4 * mc)
+
+        @pl.when(last)
+        def _():
+            for z in range(0, 16, 4):
+                VB[z : z + 4] = S0[0, 4 + z : 8 + z, 16:48, :] / MB[z : z + 4]
+
         for q in range(2):
             swaps[q].wait_recv()
             HB[4 * q : 4 * q + 4] = LB[pl.ds(8 * q + 4 * mc, 4)] + XB[4 * q : 4 * q + 4]
@@ -531,6 +548,12 @@
                 part = HB.at[pl.ds(4 * q + lax.rem(mx + d, 4), 1)]
                 pieces[q].append(remote(part, PB.at[q, d - 1], p_send.at[q, d - 1], p_recv.at[q, d - 1], along_x(d)))
             begin(pieces[q])
+
+        @pl.when(last)
+        def _():
+            begin(multiplier_moves())
+            mult_out[:, mine, :] = VB[pl.ds(4 * cy, 4)]
+
         inverse = jnp.broadcast_to(IW[...][None], (4, 8, LANES)).reshape(1, 32, LANES)
         for q in range(2):
             for c in pieces[q]:
@@ -540,48 +563,99 @@
             CB[pl.ds(own, 1)] = jnp.exp(total * inverse)
             made = CB.at[pl.ds(own, 1)]
             spread.append([remote(made, made, c_send.at[q, d - 1], c_recv.at[q, d - 1], along_x(d)) for d in (2, 1, 3)])
-            begin(spread[q])
             passed.append([])
             for d in (0, 1, 3, 2):
                 at = CB.at[pl.ds(8 * q + 4 * mc + lax.rem(mx - d + 4, 4), 1)]
                 passed[q].append((d, remote(at, at, f_send.at[q, d], f_recv.at[q, d], sibling)))
-            passed[q][0][1].start()
-            update(own)
+
+            @pl.when(jnp.logical_not(last))
+            def _():
+                begin(spread[q])
+                passed[q][0][1].start()
+                update(own)
+
+            @pl.when(last)
+            def _():
+                begin_slabs(q, own)
+
+        @pl.when(jnp.logical_not(last))
+        def _():
+            for q in range(2):
+                for (d, c), arrived in zip(passed[q][1:], spread[q][1:] + spread[q][:1]):
+                    arrived.wait_recv()
+                    c.start()
+                    update(8 * q + 4 * mc + lax.rem(mx - d + 4, 4))
+            for q in range(2):
+                for d, c in passed[q]:
+                    c.wait_recv()
+                    update(8 * q + 4 * (1 - mc) + lax.rem(mx - d + 4, 4))
+            for q in range(2):
+                for c in spread[q] + [f for _, f in passed[q]]:
+                    c.wait_send()
+
+        @pl.when(last)
+        def _():
+            finish_slabs()
+
         for q in range(2):
-            for (d, c), arrived in zip(passed[q][1:], spread[q][1:] + spread[q][:1]):
-                arrived.wait_recv()
-                c.start()
-                update(8 * q + 4 * mc + lax.rem(mx - d + 4, 4))
-        for d in range(1, 4):
-            to = lax.rem(cy + d, 4)
-            pl.when(last & (lax.rem(to, 2) == mc))(multiplier_moves()[d - 1].start)
+            for c in [swaps[q]] + pieces[q]:
+                c.wait_send()
+
+    def slab_pieces(q, own):
+        made, place = CB.at[pl.ds(own, 1)], cent_out.at[pl.ds(mx, 1), mine]
+        return [
+            remote(made, place, e_send.at[q, d], e_recv.at[d, cy], (2 * lax.rem(mx + d, 4) + mc, cz * 4 + 2 * q + mc))
+            for d in range(4)
+        ]
+
+    def begin_slabs(q, own):
+        home, copies = cy == 2 * q + mc, slab_pieces(q, own)
+        for d in (2, 1, 3):
+            copies[d].start()
+        pl.when(jnp.logical_not(home))(copies[0].start)
+
+        @pl.when(home)
+        def _():
+            cent_out[pl.ds(mx, 1), mine, :] = CB[pl.ds(own, 1)]
+
+    def finish_slabs():
+        receiver = lax.rem(cy, 2) == mc
+        sibling = (member + 1 - 2 * mc, slab)
+
+        def piece(d, e):
+            return cent_out.at[pl.ds(lax.rem(mx - d + 4, 4), 1), pl.ds(32 * e, 32)]
+
+        def passing(d, e):
+            return remote(piece(d, e), piece(d, e), k_send.at[d, e], k_recv.at[d, e], sibling)
+
+        order = [(d, e) for d in (0, 1, 3, 2) for e in range(4)]
+
+        @pl.when(receiver)
+        def _():
+            for d, e in order:
+                arrival = remote(piece(d, e), piece(d, e), e_send.at[0, d], e_recv.at[d, e], sibling)
+                if d == 0:
+                    pl.when(cy != e)(arrival.wait_recv)
+                else:
+                    arrival.wait_recv()
+                passing(d, e).start()
+            for d, e in order:
+                passing(d, e).wait_send()
+
+        @pl.when(jnp.logical_not(receiver))
+        def _():
+            for d, e in order:
+                passing(d, e).wait_recv()
+
         for q in range(2):
-            for d, c in passed[q]:
-                c.wait_recv()
-                update(8 * q + 4 * (1 - mc) + lax.rem(mx - d + 4, 4))
-        for d in range(1, 4):
-            to = lax.rem(cy + d, 4)
-            pl.when(last & (lax.rem(to, 2) != mc))(multiplier_moves()[d - 1].start)
-        pl.when(last)(lambda: begin(centroid_moves()))
-        for q in range(2):
-            for c in [swaps[q]] + pieces[q] + spread[q] + [f for _, f in passed[q]]:
-                c.wait_send()
+            copies = slab_pieces(q, 8 * q + 4 * mc + mx)
+            for d in (1, 2, 3):
+                copies[d].wait_send()
+            pl.when(cy != 2 * q + mc)(copies[0].wait_send)
+        finish(multiplier_moves())
 
     def multiplier_moves():
-        return to_slabs(S0.at[0], 4, 16, mult_out, o_send.at[1], o_recv.at[1])
-
-    def centroid_moves():
-        copies = []
-        for d in range(1, 4):
-            to = lax.rem(cy + d, 4)
-            copies.append(
-                remote(
-                    CB.at[pl.ds(4 * to + 2 * mc, 2)],
-                    cent_out.at[pl.ds(2 * mc, 2), pl.ds(pl.multiple_of(32 * cy, 32), 32)],
-                    o_send.at[0, d - 1], o_recv.at[0, d - 1], (member, cz * 4 + to),
-                )
-            )
-        return copies
+        return to_slabs(VB, 0, 0, mult_out, o_send, o_recv)
 
     def half_step(n, _):
         slot = lax.rem(n, 2)
@@ -612,14 +686,7 @@
 
     lax.fori_loop(0, 2 * ITERS, half_step, 0)
 
-    mult_out[:, mine, :] = S0[0, pl.ds(4 + 4 * cy, 4), 16:48, :]
-    cent_out[pl.ds(2 * mc, 2), mine, :] = CB[pl.ds(4 * cy + 2 * mc, 2)]
-    finish(centroid_moves())
-    half_out = cent_out.at[pl.ds(2 * mc, 2)]
-    across = remote(half_out, half_out, x_send.at[0], x_recv.at[0], (member + 1 - 2 * mc, slab))
-    across.start()
-    finish(multiplier_moves())
-    across.wait()
+    mult_out[...] = mult_out[...] * cent_out[...]
 
 
 def body(nonnegative_volumes, reaction, diffusivity, member_weights):
@@ -634,14 +701,15 @@
     scratch = [
         buffer(2, 24, 64), *[buffer(24, 64) for _ in range(7)], buffer(5, 48), buffer(10, 48),
         *[buffer(18, 40) for _ in range(8)], buffer(8, 32), buffer(8, 32), buffer(5, 24),
-        buffer(2, 2, 3, 24), buffer(2, 2, 5, 8), buffer(2, 4, 3, 8), buffer(2, 8, 8), buffer(2, 2, 8, 8), buffer(2, 4, 2, 8),
+        buffer(2, 2, 3, 24), buffer(2, 2, 5, 8), buffer(2, 4, 3, 8), buffer(2, 8, 8), buffer(2, 2, 8, 8), buffer(2, 4, 1, 8),
         buffer(2, 16, 24), buffer(4, 32), buffer(4, 32), buffer(4, 32), buffer(6, 48), buffer(4, 32), buffer(4, 32), buffer(16), buffer(6, 16),
         buffer(16, 32), buffer(16, 32), buffer(16, 32), buffer(8, 32), buffer(8, 32), buffer(2, 3, 1, 32), buffer(16, 32),
         buffer(8), buffer(8, 8), buffer(8),
         *[pltpu.VMEM(shape, BF16) for shape in ((128, 128), (512, 128), (512, 128), (128, 512), (128, 512), (128, 128))],
-        dma((2, 8)), dma((2, 8)), dma((2, 8)), dma((2, 8)), dma((2, 16)), dma((2, 16)),
+        dma((2, 8)), dma((2, 8)), dma((2, 8)), dma((2, 8)), dma((2,)), dma((2,)),
         dma((3,)), dma((3,)), dma((3,)), dma((3,)), dma((7,)), dma((7,)),
-        dma((2,)), dma((2,)), dma((2,)), *[dma((2, 3)) for _ in range(4)], dma((2, 4)), dma((2, 4)), dma((2, 3)), dma((2, 3)),
+        dma((2,)), dma((2,)), dma((2,)), *[dma((2, 3)) for _ in range(4)], dma((2, 4)), dma((2, 4)), dma((3,)), dma((3,)),
+        dma((2, 4)), dma((4, 4)), dma((4, 4)), dma((4, 4)),
     ]
     centroid, multipliers = pl.pallas_call(
         kernel,

time: 121 us -> 114 us (0.942)
  Pallas kernels: 116 us -> 108 us
    pallas_call x1, Pallas kernels: 116 us -> 108 us  [body(): pl.pallas_call(kernel, out_shape=(field, field), in_specs=[hbm, hbm, smem...]
where the time goes in v6:
time: 114 us; the launch traced here: 113 us
  Pallas kernels  108 us (95%)
  local copies, waits for them, and re-layouts  3.95 us (3%)
  between operations  1.3 us (1%)
    pallas_call x1, Pallas kernels, body(): pl.pallas_call(kernel, out_shape=(field, field), in_specs=[hbm, hbm, smem...  108 us
    unnamed x8, local copies, waits for them, and re-layouts  3.95 us

profile of v6, /device:TPU:1, one launch (start us, length us, event | category | flops | bytes accessed | tf_op | source)
XLA Modules:
  0.0 113.4 jit_solution(6775705536876346798)
XLA Ops:
  1.3 0.0 copy-start.2
  1.3 0.6 copy-done.2
  1.9 0.0 copy-start
  1.9 0.9 copy-done
  2.9 0.0 copy-start.1
  2.9 0.9 copy-done.1
  3.8 108.2 %shard_map.59 = (f32[4,128,128]{2,1,0:T(8,128)S(1)}, f32[4,128,128]{2,1,0:T(8,128)S(1)}) custom-call(f32[4,128,128]{2,1,0:T(8,128)S(1)} %bitcast.2, f32[4,128,128]{2,1,0:T(8,128)S(1)} %copy-done.1, f32[3]{0:T(128)S(1)} %copy-done.2, f32[1]{0:T(128)S(6)} %copy.8.weight_ref), custom_call_target="tpu_custom_call" | custom-call | tf_op jit(solution)/shard_map/pallas_call | solution.py:714
  112.0 0.7 copy.9
  112.7 0.7 copy.10
Async XLA Ops:
  1.3 0.7 copy-start.2
  1.9 0.9 copy-start
  2.9 0.9 copy-start.1

commit v7 on v6

--- a/solution.py
+++ b/solution.py
@@ -37,11 +37,11 @@
     S0, SC, D0, DG0, UA, UB, U0a, U0b, C0, T0,
     S1, S1C, D1, DG1, VA, VC, U1a, U1b, C1, T1, P1, LZ, LY, LD, E0, LE, LQ,
     G, S2, D2, DG2, U2, T2, C2, D3, K3,
-    VB, MB, LB, XB, HB, PB, CB, WS, WB, IW,
+    RS, RT, RG, VB, QB, MB, LB, XB, HB, PB, CB, WS, WB, IW,
     Rx, Rx1, R3, P3, E1, Px,
     h0_send, h0_recv, h1_send, h1_recv, g_send, g_recv,
     ra_send, ra_recv, va_send, va_recv, w_send, w_recv,
-    l_sem, x_send, x_recv, p_send, p_recv, c_send, c_recv, f_send, f_recv, o_send, o_recv, e_send, e_recv, k_send, k_recv,
+    l_sem, rg_sem, x_send, x_recv, p_send, p_recv, c_send, c_recv, f_send, f_recv, o_send, o_recv, e_send, e_recv, k_send, k_recv,
 ):
     member, slab = lax.axis_index("member"), lax.axis_index("slab")
     cz, cy = slab // 4, lax.rem(slab, 4)
@@ -63,6 +63,8 @@
     own_volume = pltpu.make_async_copy(vol_ref.at[:, mine], VB.at[pl.ds(4 * cy, 4)], l_sem.at[1])
     own_reaction.start()
     own_volume.start()
+    slab_reaction = pltpu.make_async_copy(reaction_ref, RS, l_sem.at[2])
+    slab_reaction.start()
 
     barrier = pltpu.get_barrier_semaphore()
     for d in FARTHEST:
@@ -102,6 +104,15 @@
     WS[...] = jnp.full((8, LANES), weight_ref[0], F32)
     for ref in (SC, UA, UB, VA, VC, S1C, U0a, U0b, U1a, U1b, U2, T1):
         ref[...] = jnp.zeros(ref.shape, F32)
+
+    slab_reaction.wait()
+    RT[0] = RS[0] + RS[1]
+    RT[1] = RS[2] + RS[3]
+    level1 = dot(flat(RT[:, pl.ds(0, 64, stride=2), :] + RT[:, pl.ds(1, 64, stride=2), :]), Rx[...])
+    RT[0, 0:64, :] = level1[0:64] + level1[64:128]
+    level2 = RT[0, pl.ds(0, 32, stride=2), :] + RT[0, pl.ds(1, 32, stride=2), :]
+    groups = jnp.concatenate([level2[8 * k : 8 * k + 8] for k in range(4)], axis=1)
+    RG[slab] = dot(jnp.concatenate([groups, groups], axis=0), Rx1[...])[0:8]
     pl.semaphore_wait(barrier, 22)
 
     def inner(dz, dy):
@@ -228,6 +239,9 @@
     reaction_moves = to_blocks(reaction_ref, S0.at[1], 4, 16, ra_send, ra_recv)
     volume_moves = to_blocks(vol_ref, VB, 0, 0, va_send, va_recv)
     begin(reaction_moves)
+    begin([
+        remote(RG.at[slab], RG.at[slab], rg_sem.at[0], rg_sem.at[1], (member, at_slab(d // 4, d % 4))) for d in FARTHEST
+    ])
     weight_moves = [
         remote(WS, WB.at[d], w_send.at[d - 1], w_recv.at[d - 1], (lax.rem(member + d, 8), slab)) for d in range(1, 8)
     ]
@@ -362,8 +376,6 @@
     begin_halo0(1)
     SC[4:20, 16:48, :] = S0[1, 4:20, 16:48, :]
     restrict0(lambda z: SC[pl.ds(z, 4), 8:56, :])
-    restrict1(lambda z: S1C[pl.ds(z, 8), 8:32, :], 1)
-    begin(gather(1))
     begin_halo1(1)
     begin(volume_moves)
     begin(weight_moves)
@@ -397,9 +409,15 @@
         D1[pl.ds(z, 2), 8:32, :] = jnp.where(inside(1, z, 2, 8, 24), OMEGA / diag, jnp.zeros((2, 24, LANES), F32))
 
     over(1, 16, 2, diag1)
-    finish_gather(1)
-    finish_gather_sends(1)
-    gathered(1)
+    tiles = RG.at[0:15]
+    pltpu.make_async_copy(tiles, tiles, rg_sem.at[1]).wait()
+    pltpu.make_async_copy(tiles, tiles, rg_sem.at[0]).wait()
+    for c in range(4):
+        for k in range(4):
+            rows = jnp.zeros((8, LANES), F32)
+            for j in range(4):
+                rows = jnp.where((lane >= 32 * j) & (lane < 32 * j + 32), lane_roll(RG[4 * c + j], 32 * (j - k)), rows)
+            S2[c, 8 * k : 8 * k + 8, :] = rows
     DG2[...] = S2[...] + center[2]
     D2[...] = OMEGA / DG2[...]
     coefficients3(OMEGA / (restrict2(S2[...]) + center[3]))
@@ -411,7 +429,7 @@
         weight_total += WB[d]
     IW[...] = 1.0 / weight_total
 
-    def vcycle(n, slot, use):
+    def vcycle(n, slot):
         UA[4:20, 16:48, :] = D0[4:20, 16:48, :] * SC[4:20, 16:48, :]
 
         def own0(z):
@@ -506,9 +524,19 @@
         over(3, 18, 3, post0a)
 
         def post0b(z):
-            use(z, sweep(0, U0a, source0, D0, z, 4, 16, 32))
-
-        over(4, 16, 4, post0b)
+            return sweep(0, U0a, source0, D0, z, 4, 16, 32)
+
+        @pl.when(slot == 0)
+        def _():
+            for z in range(4, 20, 4):
+                p = VB[z - 4 : z] / post0b(z)
+                S0[1, z : z + 4, 16:48, :] = p
+                SC[z : z + 4, 16:48, :] = p
+
+        @pl.when(slot == 1)
+        def _():
+            for z in range(4, 20, 4):
+                MB[z - 4 : z] = post0b(z)
 
     def centroid(last):
         sibling = (member + 1 - 2 * mc, slab)
@@ -519,7 +547,7 @@
             LB[pl.ds(at, 4)] = weight_ref[0] * jnp.log(m)
 
         def update(at):
-            p = S0[0, 4 + at, 16:48, :] * CB[at] / MB[at]
+            p = QB[at] * CB[at]
             S0[0, 4 + at, 16:48, :] = p
             SC[4 + at, 16:48, :] = p
 
@@ -535,11 +563,6 @@
         for q in range(2):
             marginal(8 * q + 4 * mc)
 
-        @pl.when(last)
-        def _():
-            for z in range(0, 16, 4):
-                VB[z : z + 4] = S0[0, 4 + z : 8 + z, 16:48, :] / MB[z : z + 4]
-
         for q in range(2):
             swaps[q].wait_recv()
             HB[4 * q : 4 * q + 4] = LB[pl.ds(8 * q + 4 * mc, 4)] + XB[4 * q : 4 * q + 4]
@@ -549,10 +572,13 @@
                 pieces[q].append(remote(part, PB.at[q, d - 1], p_send.at[q, d - 1], p_recv.at[q, d - 1], along_x(d)))
             begin(pieces[q])
 
+        for z in range(0, 16, 4):
+            QB[z : z + 4] = S0[0, 4 + z : 8 + z, 16:48, :] / MB[z : z + 4]
+
         @pl.when(last)
         def _():
             begin(multiplier_moves())
-            mult_out[:, mine, :] = VB[pl.ds(4 * cy, 4)]
+            mult_out[:, mine, :] = QB[pl.ds(4 * cy, 4)]
 
         inverse = jnp.broadcast_to(IW[...][None], (4, 8, LANES)).reshape(1, 32, LANES)
         for q in range(2):
@@ -655,24 +681,12 @@
         finish(multiplier_moves())
 
     def multiplier_moves():
-        return to_slabs(VB, 0, 0, mult_out, o_send, o_recv)
+        return to_slabs(QB, 0, 0, mult_out, o_send, o_recv)
 
     def half_step(n, _):
         slot = lax.rem(n, 2)
 
-        def keep(z, h):
-            MB[pl.ds(z - 4, 4)] = h
-
-        vcycle(n, slot, keep)
-
-        @pl.when(slot == 0)
-        def _():
-            def partner(z):
-                p = VB[pl.ds(z - 4, 4)] / MB[pl.ds(z - 4, 4)]
-                S0[1, pl.ds(z, 4), 16:48, :] = p
-                SC[pl.ds(z, 4), 16:48, :] = p
-
-            over(4, 16, 4, partner)
+        vcycle(n, slot)
 
         @pl.when(slot == 1)
         def _():
@@ -703,12 +717,13 @@
         *[buffer(18, 40) for _ in range(8)], buffer(8, 32), buffer(8, 32), buffer(5, 24),
         buffer(2, 2, 3, 24), buffer(2, 2, 5, 8), buffer(2, 4, 3, 8), buffer(2, 8, 8), buffer(2, 2, 8, 8), buffer(2, 4, 1, 8),
         buffer(2, 16, 24), buffer(4, 32), buffer(4, 32), buffer(4, 32), buffer(6, 48), buffer(4, 32), buffer(4, 32), buffer(16), buffer(6, 16),
-        buffer(16, 32), buffer(16, 32), buffer(16, 32), buffer(8, 32), buffer(8, 32), buffer(2, 3, 1, 32), buffer(16, 32),
+        buffer(4, 128), buffer(2, 128), buffer(16, 8),
+        buffer(16, 32), buffer(16, 32), buffer(16, 32), buffer(16, 32), buffer(8, 32), buffer(8, 32), buffer(2, 3, 1, 32), buffer(16, 32),
         buffer(8), buffer(8, 8), buffer(8),
         *[pltpu.VMEM(shape, BF16) for shape in ((128, 128), (512, 128), (512, 128), (128, 512), (128, 512), (128, 128))],
         dma((2, 8)), dma((2, 8)), dma((2, 8)), dma((2, 8)), dma((2,)), dma((2,)),
         dma((3,)), dma((3,)), dma((3,)), dma((3,)), dma((7,)), dma((7,)),
-        dma((2,)), dma((2,)), dma((2,)), *[dma((2, 3)) for _ in range(4)], dma((2, 4)), dma((2, 4)), dma((3,)), dma((3,)),
+        dma((3,)), dma((2,)), dma((2,)), dma((2,)), *[dma((2, 3)) for _ in range(4)], dma((2, 4)), dma((2, 4)), dma((3,)), dma((3,)),
         dma((2, 4)), dma((4, 4)), dma((4, 4)), dma((4, 4)),
     ]
     centroid, multipliers = pl.pallas_call(

time: 114 us -> 112 us (0.982)
  Pallas kernels: 108 us -> 106 us
    pallas_call x1, Pallas kernels: 108 us -> 106 us  [body(): pl.pallas_call(kernel, out_shape=(field, field), in_specs=[hbm, hbm, smem...]
where the time goes in v7:
time: 112 us
  Pallas kernels  106 us (95%)
  local copies, waits for them, and re-layouts  3.95 us (4%)
  between operations  1.3 us (1%)
    pallas_call x1, Pallas kernels, body(): pl.pallas_call(kernel, out_shape=(field, field), in_specs=[hbm, hbm, smem...  106 us
    unnamed x8, local copies, waits for them, and re-layouts  3.95 us

profile of v7, /device:TPU:1, one launch (start us, length us, event | category | flops | bytes accessed | tf_op | source)
XLA Modules:
  0.0 111.6 jit_solution(13942675614708009883)
XLA Ops:
  1.3 0.0 copy-start.2
  1.3 0.6 copy-done.2
  1.9 0.0 copy-start
  1.9 0.9 copy-done
  2.9 0.0 copy-start.1
  2.9 0.9 copy-done.1
  3.8 106.4 %shard_map.59 = (f32[4,128,128]{2,1,0:T(8,128)S(1)}, f32[4,128,128]{2,1,0:T(8,128)S(1)}) custom-call(f32[4,128,128]{2,1,0:T(8,128)S(1)} %bitcast.2, f32[4,128,128]{2,1,0:T(8,128)S(1)} %copy-done.1, f32[3]{0:T(128)S(1)} %copy-done.2, f32[1]{0:T(128)S(6)} %copy.8.weight_ref), custom_call_target="tpu_custom_call" | custom-call | tf_op jit(solution)/shard_map/pallas_call | solution.py:729
  110.2 0.7 copy.9
  110.9 0.7 copy.10
Async XLA Ops:
  1.3 0.7 copy-start.2
  1.9 0.9 copy-start
  2.9 0.9 copy-start.1

commit v8 on v7

--- a/solution.py
+++ b/solution.py
@@ -134,11 +134,12 @@
         return copies
 
     def begin_halo0(slot):
+        begin_near(halo0(slot)[:2])
         for edge, row in ((0, 16), (1, 44)):
             for p in range(8):
                 E0[edge, p, 0:4, :] = S0[slot, 4 + 2 * p, row : row + 4, :]
                 E0[edge, p, 4:8, :] = S0[slot, 5 + 2 * p, row : row + 4, :]
-        begin_near(halo0(slot))
+        begin_near(halo0(slot)[2:])
 
     def finish_halo0(slot):
         finish_near(halo0(slot))
@@ -683,9 +684,7 @@
     def multiplier_moves():
         return to_slabs(QB, 0, 0, mult_out, o_send, o_recv)
 
-    def half_step(n, _):
-        slot = lax.rem(n, 2)
-
+    def half_step(n, slot):
         vcycle(n, slot)
 
         @pl.when(slot == 1)
@@ -696,9 +695,13 @@
         def _():
             begin_halo0(1 - slot)
 
+
+    def iteration(i, _):
+        half_step(2 * i, 0)
+        half_step(2 * i + 1, 1)
         return 0
 
-    lax.fori_loop(0, 2 * ITERS, half_step, 0)
+    lax.fori_loop(0, ITERS, iteration, 0)
 
     mult_out[...] = mult_out[...] * cent_out[...]
 

time: 112 us -> 111 us (level)
  no operation moved by 1% of the time
where the time goes in v8:
time: 111 us
  Pallas kernels  106 us (95%)
  local copies, waits for them, and re-layouts  3.95 us (4%)
  between operations  1.3 us (1%)
    pallas_call x1, Pallas kernels, body(): pl.pallas_call(kernel, out_shape=(field, field), in_specs=[hbm, hbm, smem...  106 us
    unnamed x8, local copies, waits for them, and re-layouts  3.95 us

profile of v8, /device:TPU:1, one launch (start us, length us, event | category | flops | bytes accessed | tf_op | source)
XLA Modules:
  0.0 110.9 jit_solution(9828809476829847864)
XLA Ops:
  1.3 0.0 copy-start.2
  1.3 0.6 copy-done.2
  1.9 0.0 copy-start
  1.9 0.9 copy-done
  2.9 0.0 copy-start.1
  2.9 0.9 copy-done.1
  3.8 105.6 %shard_map.59 = (f32[4,128,128]{2,1,0:T(8,128)S(1)}, f32[4,128,128]{2,1,0:T(8,128)S(1)}) custom-call(f32[4,128,128]{2,1,0:T(8,128)S(1)} %bitcast.2, f32[4,128,128]{2,1,0:T(8,128)S(1)} %copy-done.1, f32[3]{0:T(128)S(1)} %copy-done.2, f32[1]{0:T(128)S(6)} %copy.8.weight_ref), custom_call_target="tpu_custom_call" | custom-call | tf_op jit(solution)/shard_map/pallas_call | solution.py:732
  109.5 0.7 copy.9
  110.2 0.7 copy.10
Async XLA Ops:
  1.3 0.7 copy-start.2
  1.9 0.9 copy-start
  2.9 0.9 copy-start.1

commit v9 on v8

--- a/solution.py
+++ b/solution.py
@@ -320,7 +320,9 @@
 
     def restrict2(a):
         T2[...] = a
-        e = T2[:, pl.ds(0, 16, stride=2), :] + T2[:, pl.ds(1, 16, stride=2), :]
+        even = T2[:, pl.ds(0, 8, stride=4), :] + T2[:, pl.ds(1, 8, stride=4), :]
+        odd = T2[:, pl.ds(2, 8, stride=4), :] + T2[:, pl.ds(3, 8, stride=4), :]
+        e = jnp.concatenate([even, odd], axis=1)
         return dot(jnp.concatenate([e[0], e[1], e[2], e[3]], axis=1), R3[...])
 
     first_chunk, last_chunk = lane < 32, lane >= 96
@@ -342,7 +344,7 @@
 
     row16 = lax.broadcasted_iota(jnp.int32, (16, LANES), 0)
     zeros16, ones16 = jnp.zeros((16, LANES), F32), jnp.ones((16, LANES), F32)
-    up3 = jnp.where(row16 > 0, ones16, zeros16) * coupling[3][1]
+    up3 = jnp.where(row16 != 0, ones16, zeros16) * coupling[3][1]
     down3 = jnp.where(row16 < 15, ones16, zeros16) * coupling[3][1]
     before3 = lane_mask(lane >= 16) * coupling[3][0]
     after3 = lane_mask(lane < 112) * coupling[3][0]
@@ -358,7 +360,10 @@
         u = base
         for _ in range(COARSE_SWEEPS - 1):
             z = k[0] * lane_roll(u, 16) + k[1] * lane_roll(u, -16)
-            y = k[2] * pltpu.roll(u, 1, 0) + k[3] * pltpu.roll(u, 15, 0)
+            even, odd = u[0:8], u[8:16]
+            above = jnp.concatenate([pltpu.roll(odd, 1, 0), even], axis=0)
+            below = jnp.concatenate([odd, pltpu.roll(even, 7, 0)], axis=0)
+            y = k[2] * above + k[3] * below
             x = k[4] * lane_roll(u, 1) + k[5] * lane_roll(u, -1)
             u = (base + (1.0 - OMEGA) * u + y) + (z + x)
         return u
@@ -479,8 +484,9 @@
         u3 = level3(restrict2(S2[...] - DG2[...] * mid + total))
         p = dot(u3, P3[...])
         for k in range(4):
-            C2[k, pl.ds(0, 16, stride=2), :] = p[:, LANES * k : LANES * k + LANES]
-            C2[k, pl.ds(1, 16, stride=2), :] = p[:, LANES * k : LANES * k + LANES]
+            for i in range(4):
+                r = 8 * (i // 2)
+                C2[k, pl.ds(i, 8, stride=4), :] = p[r : r + 8, LANES * k : LANES * k + LANES]
         U2[1:5, 8:40, :] += C2[...]
         sweep2()
         sweep2()

time: 111 us -> 111 us (level)
  no operation moved by 1% of the time
where the time goes in v9:
time: 111 us
  Pallas kernels  106 us (95%)
  local copies, waits for them, and re-layouts  3.95 us (4%)
  between operations  1.3 us (1%)
    pallas_call x1, Pallas kernels, body(): pl.pallas_call(kernel, out_shape=(field, field), in_specs=[hbm, hbm, smem...  106 us
    unnamed x8, local copies, waits for them, and re-layouts  3.95 us

profile of v9, /device:TPU:1, one launch (start us, length us, event | category | flops | bytes accessed | tf_op | source)
XLA Modules:
  0.0 111.1 jit_solution(16636752695143146619)
XLA Ops:
  1.3 0.0 copy-start.2
  1.3 0.6 copy-done.2
  1.9 0.0 copy-start
  1.9 0.9 copy-done
  2.9 0.0 copy-start.1
  2.9 0.9 copy-done.1
  3.8 105.8 %shard_map.59 = (f32[4,128,128]{2,1,0:T(8,128)S(1)}, f32[4,128,128]{2,1,0:T(8,128)S(1)}) custom-call(f32[4,128,128]{2,1,0:T(8,128)S(1)} %bitcast.2, f32[4,128,128]{2,1,0:T(8,128)S(1)} %copy-done.1, f32[3]{0:T(128)S(1)} %copy-done.2, f32[1]{0:T(128)S(6)} %copy.8.weight_ref), custom_call_target="tpu_custom_call" | custom-call | tf_op jit(solution)/shard_map/pallas_call | solution.py:738
  109.7 0.7 copy.9
  110.4 0.7 copy.10
Async XLA Ops:
  1.3 0.7 copy-start.2
  1.9 0.9 copy-start
  2.9 0.9 copy-start.1
